TPU v7x, 256 devices: a whole 4x4x8 slice. The times are simulated.
256 devices in a mesh: ed: 32 (over y, z), tp: 8 (over x, core).
Axes of the slice: x: 4, y: 4, z: 8, core: 2. Of those that a mesh axis runs over, the one named last changes fastest.
Arguments:
- tokens: bfloat16 [1024, 6144], P('ed'), may hold values from -6 to 6
- expert_ids: int32 [1024, 2], P('ed'), may hold values from 0 to 3, all different within a row; in each aligned block of 32 rows (0 to 31, 32 to 63, ...) at most 24 rows name the same one
- router_logits: float32 [1024, 4], P('ed'), may hold values from -6 to 6
- gate_weight: bfloat16 [32, 6144, 2048], P('ed', None, 'tp'), may hold values from -0.078125 to 0.078125
- up_weight: bfloat16 [32, 6144, 2048], P('ed', None, 'tp'), may hold values from -0.078125 to 0.078125
- down_weight: bfloat16 [32, 2048, 6144], P('ed', 'tp'), may hold values from -0.046875 to 0.046875
Outputs:
- mixed: bfloat16 [1024, 6144], P('ed', 'tp')
Inputs may be any that keep to these rules, and one draw needn't show every extreme that they name: `expert_ids`: each row names two different experts. Among the 32 rows of one device no expert is named by more than 24 rows, and in every draw some expert is named by exactly 24 rows of some device.
All inputs are finite; a program needn't handle non-finite values.
Results may differ from a plain program's by a relative error of at most 0.0049.
Values may be sent and summed in bfloat16 or wider, within the bound.
A program may use at most 128 MiB of HBM per device.

v0:
```python
import jax
import jax.numpy as jnp
from jax import lax
from jax.sharding import PartitionSpec as P

FF = 16384
EXPERTS = 4


def from_partner(block, axis, distance):
    count = lax.axis_size(axis)
    route = []
    for low in range(count):
        high = low | 1 << distance
        if high != low and high < count:
            route += [(low, high), (high, low)]
    return lax.ppermute(block, axis, route)


def sylvester(order_size):
    indices = jnp.arange(order_size, dtype=jnp.int32)
    intersection = indices[:, None] & indices[None, :]
    parity = jnp.zeros((order_size, order_size), jnp.int32)
    for segment in range(max(order_size.bit_length(), 1)):
        parity = parity ^ intersection >> segment & 1
    return (1 - 2 * parity).astype(jnp.float32)


def on_device(tokens, expert_ids, router_logits, gate_weight, up_weight, down_weight):
    ed_count = lax.axis_size("ed")
    tp_count = lax.axis_size("tp")
    group_size = ed_count // EXPERTS
    tok_count = tokens.shape[0]
    capacity = tok_count * 3 // 4
    model_width = tokens.shape[1]
    ed_index = lax.axis_index("ed")
    tp_index = lax.axis_index("tp")
    expert_range = jnp.arange(EXPERTS, dtype=jnp.int32)
    picked = expert_ids[:, :, None] == expert_range[None, None, :]
    chosen = jnp.any(picked, axis=1).astype(jnp.int32)
    slot_index = jnp.cumsum(chosen, axis=0) - chosen
    slot_range = jnp.arange(capacity, dtype=jnp.int32)
    placing = (chosen[:, :, None] == 1) & (slot_index[:, :, None] == slot_range[None, None, :])
    packed = jnp.einsum(
        "tem,td->emd", placing.astype(jnp.bfloat16), tokens, preferred_element_type=jnp.float32
    ).astype(jnp.bfloat16)
    outgoing = jnp.repeat(packed, group_size, axis=0)
    arrived = lax.all_to_all(outgoing, "ed", split_axis=0, concat_axis=0, tiled=True)
    routed = arrived.reshape(-1, model_width)
    gate_act = jnp.dot(routed, gate_weight[0], preferred_element_type=jnp.float32)
    up_act = jnp.dot(routed, up_weight[0], preferred_element_type=jnp.float32)
    hidden = jax.nn.silu(gate_act) * up_act
    units = hidden.shape[1]
    mixed_units = jnp.dot(hidden, sylvester(units), precision=lax.Precision.HIGHEST)
    for segment in range(group_size.bit_length() - 1):
        partner = from_partner(mixed_units, "ed", segment)
        is_upper = ed_index >> segment & 1 == 1
        mixed_units = jnp.where(is_upper, partner - mixed_units, mixed_units + partner)
    for segment in range(tp_count.bit_length() - 1):
        partner = from_partner(mixed_units, "tp", segment)
        is_upper = tp_index >> segment & 1 == 1
        mixed_units = jnp.where(is_upper, partner - mixed_units, mixed_units + partner)
    rotated = (mixed_units * FF ** (-0.5)).astype(jnp.bfloat16)
    down_rows = down_weight[0]
    partial_value = lax.psum_scatter(
        lax.dot_general(
            down_rows, rotated, (((0,), (1,)), ((), ())), preferred_element_type=jnp.float32
        ),
        "tp",
        scatter_dimension=0,
        tiled=True,
    )
    returned = lax.all_to_all(partial_value, "ed", split_axis=1, concat_axis=1, tiled=True)
    feature_rows = returned.shape[0]
    summed = returned.reshape(feature_rows, EXPERTS, group_size, capacity).sum(axis=2)
    summed = summed.reshape(feature_rows, EXPERTS * capacity)
    picked_logits = jnp.sum(jnp.where(picked, router_logits[:, None, :], 0.0), axis=2)
    first_share = 1.0 / (1.0 + jnp.exp(picked_logits[:, 1] - picked_logits[:, 0]))
    shares = jnp.stack([first_share, 1.0 - first_share], axis=1)
    weight_e = jnp.sum(jnp.where(picked, shares[:, :, None], 0.0), axis=1)
    combine = jnp.where(placing, weight_e[:, :, None], 0.0).reshape(tok_count, EXPERTS * capacity)
    output = lax.dot_general(
        combine, summed, (((1,), (1,)), ((), ())), precision=lax.Precision.HIGHEST
    )
    return output.astype(jnp.bfloat16)


def solution(mesh):
    placed = (
        P("ed", None),
        P("ed", None),
        P("ed", None),
        P("ed", None, "tp"),
        P("ed", None, "tp"),
        P("ed", "tp", None),
    )
    return jax.shard_map(
        on_device, mesh=mesh, in_specs=placed, out_specs=P("ed", "tp"), check_vma=False
    )
```

profile of v0, /device:TPU:8, one launch (start us, length us, event | category | flops | bytes accessed | tf_op | source)
XLA Modules:
  0.0 569.8 jit_solution(2166521545728371419)
XLA Ops:
  10.4 217.6 %all_to_all.14 = bf16[32,24,6144]{2,1,0:T(8,128)(2,1)S(1)} all-to-all(bf16[32,24,6144]{2,1,0:T(8,128)(2,1)S(1)} %bitcast.29), channel_id=1, replica_groups=mesh['ed'=32,'tp'=8] {'ed'}, dimensions={0} | all-to-all | bytes 18874368 | tf_op jit(solution)/shard_map/all_to_all | solution.py:48
  228.0 2.6 fusion.3
  230.6 2.6 fusion.5
  233.2 1.9 fusion.12
  235.1 3.1 collective-permute-start
  238.2 16.8 %collective-permute-done = f32[768,256]{1,0:T(8,128)} collective-permute-done((f32[768,256]{1,0:T(8,128)}, f32[768,256]{1,0:T(8,128)}, u32[]{:S(2)}, u32[]{:S(2)}) %collective-permute-start) | collective-permute-done | bytes 786464 | tf_op jit(solution)/shard_map/ppermute | solution.py:17
  255.0 2.4 add_select_fusion.4
  258.2 34.9 %collective-permute-done.1 = f32[768,256]{1,0:T(8,128)} collective-permute-done((f32[768,256]{1,0:T(8,128)}, f32[768,256]{1,0:T(8,128)}, u32[]{:S(2)}, u32[]{:S(2)}) %collective-permute-start.1) | collective-permute-done | bytes 786464 | tf_op jit(solution)/shard_map/ppermute | solution.py:17
  293.0 2.4 add_select_fusion.3
  295.4 3.3 collective-permute-start.2
  298.7 36.1 %collective-permute-done.2 = f32[768,256]{1,0:T(8,128)} collective-permute-done((f32[768,256]{1,0:T(8,128)}, f32[768,256]{1,0:T(8,128)}, u32[]{:S(2)}, u32[]{:S(2)}) %collective-permute-start.2) | collective-permute-done | bytes 786464 | tf_op jit(solution)/shard_map/ppermute | solution.py:17
  334.8 2.4 add_select_fusion.2
  337.2 2.6 collective-permute-done.3
  339.8 2.4 add_select_fusion.1
  342.2 1.5 collective-permute-start.4
  343.7 18.4 %collective-permute-done.4 = f32[768,256]{1,0:T(8,128)} collective-permute-done((f32[768,256]{1,0:T(8,128)}, f32[768,256]{1,0:T(8,128)}, u32[]{:S(2)}, u32[]{:S(2)}) %collective-permute-start.4) | collective-permute-done | bytes 786464 | tf_op jit(solution)/shard_map/ppermute | solution.py:17
  362.1 2.4 add_select_fusion
  364.4 3.0 collective-permute-start.5
  367.5 17.5 %collective-permute-done.5 = f32[768,256]{1,0:T(8,128)} collective-permute-done((f32[768,256]{1,0:T(8,128)}, f32[768,256]{1,0:T(8,128)}, u32[]{:S(2)}, u32[]{:S(2)}) %collective-permute-start.5) | collective-permute-done | bytes 786464 | tf_op jit(solution)/shard_map/ppermute | solution.py:17
  385.0 9.3 %convolution_bitcast_fusion = f32[6144,768]{0,1:T(8,128)} fusion(bf16[1,256,6144]{2,1,0:T(8,128)(2,1)S(1)} %copy-done, f32[768,256]{1,0:T(8,128)} %add_select_fusion, f32[768,256]{1,0:T(8,128)} %collective-permute-done.5, pred[]{:T(512)S(6)} %eq.63), kind=kOutput, calls=%fused_computation | convolution fusion | flops 2416902144 | bytes 23592960 | tf_op jit(solution)/shard_map/dot_general | solution.py:66
  394.3 102.2 %reduce-scatter.2.cloned.1.call-done = f32[768,768]{0,1:T(8,128)} async-done(((f32[6144,768]{0,1:T(8,128)}), f32[768,768]{0,1:T(8,128)}) %reduce-scatter.2.cloned.1.call-update) | async-done | bytes 2359312 | tf_op jit(solution)/shard_map/reduce_scatter | solution.py:65
  496.5 10.2 %all-to-all-start.1 = ((f32[768,32,24]{0,2,1:T(8,128)}), f32[768,32,24]{0,2,1:T(8,128)}, u32[]{:S(2)}, u32[]{:S(2)}) async-start(f32[768,32,24]{0,2,1:T(8,128)} %bitcast.32), calls=%async_computation.2 | async-start | bytes 4718592 | tf_op jit(solution)/shard_map/all_to_all | solution.py:73
  506.8 53.4 %all-to-all-done.1 = f32[768,32,24]{0,2,1:T(8,128)} async-done(((f32[768,32,24]{0,2,1:T(8,128)}), f32[768,32,24]{0,2,1:T(8,128)}, u32[]{:S(2)}, u32[]{:S(2)}) %all-to-all-start.1) | async-done | bytes 2359328 | tf_op jit(solution)/shard_map/all_to_all | solution.py:73
  560.2 1.8 bitcast_reduce_fusion
  (28 shorter events, 5.7 us)
Async XLA Ops:
  6.5 378.5 %copy-start = (bf16[1,256,6144]{2,1,0:T(8,128)(2,1)S(1)}, bf16[1,256,6144]{2,1,0:T(8,128)(2,1)}, u32[]{:S(2)}) copy-start(bf16[1,256,6144]{2,1,0:T(8,128)(2,1)} %param.11) | copy-start | bytes 9437188
  6.5 490.0 %reduce-scatter.2.cloned.1.call-start = ((), (), s32[]{:S(2)}) async-start(), calls=%async_computation.3 | async-start | bytes 21233664 | tf_op jit(solution)/shard_map/reduce_scatter | solution.py:65
  10.3 217.6 %copy-start.3 = (bf16[1,6144,256]{2,1,0:T(8,128)(2,1)S(1)}, bf16[1,6144,256]{2,1,0:T(8,128)(2,1)}, u32[]{:S(2)}) copy-start(bf16[1,6144,256]{2,1,0:T(8,128)(2,1)} %param.9) | copy-start | bytes 9437188
  228.0 2.6 copy-start.4
  235.1 19.9 %collective-permute-start = (f32[768,256]{1,0:T(8,128)}, f32[768,256]{1,0:T(8,128)}, u32[]{:S(2)}, u32[]{:S(2)}) collective-permute-start(f32[768,256]{1,0:T(8,128)} %fusion.12), channel_id=1, source_target_pairs={{0,8},{8,0},{16,24},{24,16},{32,40},{40,32},{48,56},{56,48},{64,72... | collective-permute-start | bytes 2359304 | tf_op jit(solution)/shard_map/ppermute | solution.py:17
  257.4 35.7 %collective-permute-start.1 = (f32[768,256]{1,0:T(8,128)}, f32[768,256]{1,0:T(8,128)}, u32[]{:S(2)}, u32[]{:S(2)}) collective-permute-start(f32[768,256]{1,0:T(8,128)} %add_select_fusion.4), channel_id=1, source_target_pairs={{0,16},{16,0},{8,24},{24,8},{32,48},{48,32},{40,56},{56,40},{64,80... | collective-permute-start | bytes 2359304 | tf_op jit(solution)/shard_map/ppermute | solution.py:17
  295.4 39.5 %collective-permute-start.2 = (f32[768,256]{1,0:T(8,128)}, f32[768,256]{1,0:T(8,128)}, u32[]{:S(2)}, u32[]{:S(2)}) collective-permute-start(f32[768,256]{1,0:T(8,128)} %add_select_fusion.3), channel_id=1, source_target_pairs={{0,32},{32,0},{8,40},{40,8},{16,48},{48,16},{24,56},{56,24},{64,96... | collective-permute-start | bytes 2359304 | tf_op jit(solution)/shard_map/ppermute | solution.py:17
  337.2 2.6 collective-permute-start.3
  342.2 19.9 %collective-permute-start.4 = (f32[768,256]{1,0:T(8,128)}, f32[768,256]{1,0:T(8,128)}, u32[]{:S(2)}, u32[]{:S(2)}) collective-permute-start(f32[768,256]{1,0:T(8,128)} %add_select_fusion.1), channel_id=1, source_target_pairs={{0,2},{2,0},{1,3},{3,1},{4,6},{6,4},{5,7},{7,5},{8,10},{10,8},{9,1... | collective-permute-start | bytes 2359304 | tf_op jit(solution)/shard_map/ppermute | solution.py:17
  364.4 20.6 %collective-permute-start.5 = (f32[768,256]{1,0:T(8,128)}, f32[768,256]{1,0:T(8,128)}, u32[]{:S(2)}, u32[]{:S(2)}) collective-permute-start(f32[768,256]{1,0:T(8,128)} %add_select_fusion), channel_id=1, source_target_pairs={{0,4},{4,0},{1,5},{5,1},{2,6},{6,2},{3,7},{7,3},{8,12},{12,8},{9,1... | collective-permute-start | bytes 2359304 | tf_op jit(solution)/shard_map/ppermute | solution.py:17
  394.3 112.4 %copy-start.1 = (s32[32,2]{0,1:T(2,128)S(1)}, s32[32,2]{0,1:T(2,128)}, u32[]{:S(2)}) copy-start(s32[32,2]{0,1:T(2,128)} %param.7) | copy-start | bytes 772
  394.3 112.4 %copy-start.2 = (f32[32,4]{0,1:T(4,128)S(1)}, f32[32,4]{0,1:T(4,128)}, u32[]{:S(2)}) copy-start(f32[32,4]{0,1:T(4,128)} %param.8) | copy-start | bytes 1540
  496.5 63.7 %all-to-all-start.1 = ((f32[768,32,24]{0,2,1:T(8,128)}), f32[768,32,24]{0,2,1:T(8,128)}, u32[]{:S(2)}, u32[]{:S(2)}) async-start(f32[768,32,24]{0,2,1:T(8,128)} %bitcast.32), calls=%async_computation.2 | async-start | bytes 4718592 | tf_op jit(solution)/shard_map/all_to_all | solution.py:73
Sparse Core Ops, SparseCore 0:
  394.4 102.0 reduce-scatter.1
where the time goes:
time: 573 us; the launch traced here: 570 us
  waiting for transfers between devices  282 us (49%)
  blocking collectives  218 us (38%)
  starting transfers between devices  22 us (4%)
  matrix products  18.8 us (3%)
  other arithmetic  14.6 us (3%)
  between operations  13.5 us (2%)
    all_to_all x1, blocking collectives, on_device(): lax.all_to_all(outgoing, 'ed', split_axis=0, concat_axis=0, tiled=True)  218 us
    ppermute x6, waiting for transfers between devices, from_partner(): return lax.ppermute(block, axis, route)  126 us
    reduce_scatter x1, waiting for transfers between devices, on_device(): lax.psum_scatter(lax.dot_general(down_rows, rotated, (((0,), (1,)), ((),...  102 us
    all_to_all x1, waiting for transfers between devices, on_device(): lax.all_to_all(partial_value, 'ed', split_axis=1, concat_axis=1, tiled=True)  53.4 us
    ppermute x6, starting transfers between devices, from_partner(): return lax.ppermute(block, axis, route)  11.8 us
    select_n x5, other arithmetic, on_device(): jnp.where(is_upper, partner - mixed_units, mixed_units + partner)  11.8 us
  transfers between devices with their start and end apart: 8, of which 8 were waited for; matrix products, arithmetic and copies ran while one was open for 0% of the time, Pallas kernels for 0%

commit v1 on v0

v1 whole, which is shorter than its diff:
```python
import jax
import jax.numpy as jnp
from jax import lax
from jax.experimental import pallas as pl
from jax.experimental.pallas import tpu as pltpu
from jax.sharding import PartitionSpec as P

MESH = pl.DeviceIdType.MESH
BF16, F32 = jnp.bfloat16, jnp.float32
D = 6144
FF = 16384
EXPERTS = 4
TOK = 32
CAP = 24
NX, NY, NZ = 4, 4, 8
BLK = EXPERTS * CAP
PW = 384
PARTS = D // PW
UNITS = 256
SLICE = 768
HALF = PARTS // 2


def mod(value, count):
    return lax.rem(value + count, count)


def kernel(
    packed, gate_hbm, up_hbm, down_hbm, out,
    gate, up, down, had, ybuf, rows, core_s, core_r, a2a_s, a2a_r, back_s, rot,
    own, sib_s, sib_r, xs, xr, zs, zr, fxs, fxr, ys, yr,
    w_sem, y_ss, y_rs, z_ss, z_rs, x_ss, x_rs, s_ss, s_rs, c_ss, c_rs, a_ss, a_rs, b_ss, b_rs,
    sib_ss, sib_rs, x3_ss, x3_rs, z3_ss, z3_rs, fx_ss, fx_rs, y3_ss, y3_rs,
):
    ed, tp = lax.axis_index("ed"), lax.axis_index("tp")
    y, z = lax.div(ed, NZ), lax.rem(ed, NZ)
    x, c = lax.div(tp, 2), lax.rem(tp, 2)

    def at(x=x, y=y, z=z, c=c):
        return (y * NZ + z, x * 2 + c)

    sibling = at(c=1 - c)
    x_peer = [mod(x + i, NX) for i in range(NX)]
    y_peer = [mod(y + i, NY) for i in range(NY)]
    step_to = (at(z=mod(z + 1, NZ)), at(z=mod(z - 1, NZ)))

    def remote(src, dst, send, recv, device):
        return pltpu.make_async_remote_copy(
            src_ref=src, dst_ref=dst, send_sem=send, recv_sem=recv, device_id=device, device_id_type=MESH
        )

    sent = []

    def push(src, dst, send, recv, device):
        copy = remote(src, dst, send, recv, device)
        copy.start()
        sent.append(copy)

    def arrive(dst, send, recv):
        remote(dst, dst, send, recv, sibling).wait_recv()

    weights = [
        pltpu.make_async_copy(gate_hbm.at[0], gate, w_sem.at[0]),
        pltpu.make_async_copy(up_hbm.at[0], up, w_sem.at[1]),
        pltpu.make_async_copy(down_hbm.at[0], down, w_sem.at[2]),
    ]
    for copy in weights:
        copy.start()

    barrier = pltpu.get_barrier_semaphore()
    greeted = [sibling, *step_to]
    greeted += [at(x=x_peer[i]) for i in range(1, NX)]
    greeted += [at(y=y_peer[i]) for i in range(1, NY)]
    for device in greeted:
        pl.semaphore_signal(barrier, inc=1, device_id=device, device_id_type=MESH)
    pl.semaphore_wait(barrier, len(greeted))

    base = c * HALF
    wide, narrow = 4 * PW, PW
    shared = base + 4 + x
    cols_wide = pl.ds(pl.multiple_of(base * PW, 128), wide)
    cols_narrow = pl.ds(pl.multiple_of(shared * PW, 128), narrow)
    for i in (2, 1, 3):
        slot = pl.ds(pl.multiple_of(y_peer[i] * TOK, TOK), TOK)
        device = at(y=y_peer[i])
        push(packed.at[slot, cols_narrow], ybuf.at[y, :, pl.ds(wide, narrow)], y_ss.at[i, 0], y_rs.at[i, 0], device)
        push(packed.at[slot, cols_wide], ybuf.at[y, :, pl.ds(0, wide)], y_ss.at[i, 1], y_rs.at[i, 1], device)
    slot = pl.ds(pl.multiple_of(y * TOK, TOK), TOK)
    ybuf[y, :, 0:wide] = packed[slot, cols_wide]
    ybuf[y, :, wide:] = packed[slot, cols_narrow]

    both = lax.broadcasted_iota(jnp.int32, (UNITS, UNITS), 0) & lax.broadcasted_iota(jnp.int32, (UNITS, UNITS), 1)
    for shift in (4, 2, 1):
        both = both ^ (both >> shift)
    had[...] = (1 - 2 * (both & 1)).astype(F32).astype(BF16)

    i_row = lax.broadcasted_iota(jnp.int32, (BLK, NY * TOK), 0)
    i_col = lax.broadcasted_iota(jnp.int32, (BLK, NY * TOK), 1)
    squeeze = jnp.zeros((BLK, NY * TOK), F32)
    for s in range(NY):
        inside = (i_row >= CAP * s) & (i_row < CAP * (s + 1)) & (i_col - TOK * s == i_row - CAP * s)
        squeeze = jnp.where(inside, 1.0, squeeze)
    squeeze = squeeze.astype(BF16)

    for i in range(1, NY):
        source = y_peer[NY - i]
        arrive(ybuf.at[source, :, pl.ds(wide, narrow)], y_ss.at[i, 0], y_rs.at[i, 0])
        arrive(ybuf.at[source, :, pl.ds(0, wide)], y_ss.at[i, 1], y_rs.at[i, 1])

    def squeezed(at_col):
        block = ybuf[:, :, at_col:at_col + PW].reshape(NY * TOK, PW)
        return jnp.dot(squeeze, block, preferred_element_type=F32).astype(BF16)

    rows[z, shared] = squeezed(wide)
    for p in range(4):
        rows[z, base + p] = squeezed(p * PW)

    blocks = [z]
    for t in (1, 2, 3):
        blocks += [mod(z - t, NZ), mod(z + t, NZ)]
    blocks.append(mod(z + 4, NZ))

    def z_send(b, way, t):
        if t < 4:
            push(rows.at[b, shared], rows.at[b, shared], z_ss.at[way, t, 0], z_rs.at[way, t, 0], step_to[way])
            part = rows.at[b, pl.ds(base, 4)]
        elif way == 0:
            push(rows.at[b, shared], rows.at[b, shared], z_ss.at[way, t, 0], z_rs.at[way, t, 0], step_to[way])
            part = rows.at[b, pl.ds(base, 2)]
        else:
            part = rows.at[b, pl.ds(base + 2, 2)]
        push(part, part, z_ss.at[way, t, 1], z_rs.at[way, t, 1], step_to[way])

    def share(b, i):
        for j in (2, 1, 3):
            push(rows.at[b, shared], rows.at[b, shared], x_ss.at[i, j], x_rs.at[i, j], at(x=x_peer[j]))
        push(rows.at[b, shared], rows.at[b, shared], s_ss.at[i, 0], s_rs.at[i, 0], sibling)
        part = rows.at[b, pl.ds(base, 4)]
        push(part, part, s_ss.at[i, 4], s_rs.at[i, 4], sibling)

    def x_pass(b, i):
        for j in (1, 3, 2):
            part = rows.at[b, base + 4 + x_peer[NX - j]]
            arrive(part, x_ss.at[i, j], x_rs.at[i, j])
            push(part, part, s_ss.at[i, j], s_rs.at[i, j], sibling)

    other = (1 - c) * HALF

    def ready(b, i):
        part = rows.at[b, pl.ds(other, 4)]
        arrive(part, s_ss.at[i, 4], s_rs.at[i, 4])
        for j in range(NX):
            part = rows.at[b, other + 4 + x_peer[(NX - j) % NX]]
            arrive(part, s_ss.at[i, j], s_rs.at[i, j])

    def hidden(b):
        gate_act = jnp.zeros((BLK, UNITS), F32)
        up_act = jnp.zeros((BLK, UNITS), F32)
        for p in range(0, PARTS, 2):
            block = jnp.concatenate([rows[b, p], rows[b, p + 1]], axis=1)
            gate_act += jnp.dot(block, gate[p * PW:(p + 2) * PW, :], preferred_element_type=F32)
            up_act += jnp.dot(block, up[p * PW:(p + 2) * PW, :], preferred_element_type=F32)
        value = gate_act / (1.0 + jnp.exp(-gate_act)) * up_act
        high = value.astype(BF16)
        low = (value - high.astype(F32)).astype(BF16)
        core_s[b] = jnp.dot(high, had[...], preferred_element_type=F32) + jnp.dot(
            low, had[...], preferred_element_type=F32
        )

    def core_push(b, i):
        push(core_s.at[b], core_r.at[b], c_ss.at[i], c_rs.at[i], sibling)

    sign = (1 - 2 * c).astype(F32)
    me32 = z * NX + x

    def spread(b, i):
        arrive(core_r.at[b], c_ss.at[i], c_rs.at[i])
        value = (core_r[b] + sign * core_s[b]).astype(BF16)
        for k in range(NX):
            a2a_s[b, k] = value[48 * (k // 2):48 * (k // 2) + 48, 128 * (k % 2):128 * (k % 2) + 128]
        for j in range(NX):
            k = x_peer[j]
            if i == 0 and j == 0:
                a2a_r[me32] = a2a_s[b, k]
            else:
                push(a2a_s.at[b, k], a2a_r.at[me32], a_ss.at[i, j], a_rs.at[0], at(x=k, z=b))

    for way in (0, 1):
        z_send(z, way, 1)
    share(z, 0)

    for copy in weights[:2]:
        copy.wait()

    def group(t):
        if t == 0:
            return [0]
        return [2 * t - 1, 2 * t] if t < 4 else [7]

    for t in (1, 2, 3, 4):
        for way in (0, 1):
            i = group(t)[way] if t < 4 else 7
            b = blocks[i]
            if t < 4 or way == 0:
                arrive(rows.at[b, shared], z_ss.at[way, t, 0], z_rs.at[way, t, 0])
            if t < 4:
                part = rows.at[b, pl.ds(base, 4)]
            else:
                part = rows.at[b, pl.ds(base + 2 * way, 2)]
            arrive(part, z_ss.at[way, t, 1], z_rs.at[way, t, 1])
            if t < 4:
                z_send(b, way, t + 1)
        for i in group(t):
            share(blocks[i], i)
        for i in group(t - 1):
            x_pass(blocks[i], i)
        if t >= 2:
            for i in group(t - 2):
                spread(blocks[i], i)
        for i in group(t - 1):
            ready(blocks[i], i)
            hidden(blocks[i])
            core_push(blocks[i], i)
    x_pass(blocks[7], 7)
    for i in group(3):
        spread(blocks[i], i)
    ready(blocks[7], 7)
    hidden(blocks[7])
    core_push(blocks[7], 7)
    spread(blocks[7], 7)

    remote(a2a_r.at[pl.ds(0, 31)], a2a_r.at[pl.ds(0, 31)], a_ss.at[0, 0], a_rs.at[0], sibling).wait_recv()
    count = NZ * NX

    @pl.loop(0, 3)
    def _(r):
        piece = pl.ds(pl.multiple_of(r * 16, 16), 16)
        values = [a2a_r[s, piece, :].astype(F32) for s in range(count)]
        stride = 1
        while stride < count:
            for low in range(count):
                if low & stride == 0:
                    first, second = values[low], values[low + stride]
                    values[low], values[low + stride] = first + second, first - second
            stride *= 2
        for s in range(count):
            back_s[s, piece, :] = (values[s] * FF ** -0.5).astype(BF16)

    rot[z, x] = back_s[me32]
    for dz in (4, 3, 5, 2, 6, 1, 7, 0):
        zz = mod(z + dz, NZ)
        for j in range(NX):
            if dz + j:
                s = zz * NX + x_peer[j]
                push(back_s.at[s], rot.at[z, x], b_ss.at[dz, j], b_rs.at[z], at(x=x_peer[j], z=zz))

    weights[2].wait()
    order = [4, 3, 5, 2, 6, 1, 7, 0]
    x3_parts = [mod(x + i, NX) for i in range(NX)]

    def down_block(dz, turn):
        b = mod(z + dz, NZ)
        if dz:
            arrive(rot.at[b], b_ss.at[0, 1], b_rs.at[b])
        else:
            arrive(rot.at[b, pl.ds(0, 3)], b_ss.at[0, 1], b_rs.at[b])
        upper = jnp.concatenate([rot[b, 0], rot[b, 1]], axis=1)
        lower = jnp.concatenate([rot[b, 2], rot[b, 3]], axis=1)
        block = jnp.concatenate([upper, lower], axis=0)
        slot = turn % 2
        if turn >= 2:
            remote(sib_s.at[slot], sib_r.at[b], sib_ss.at[slot], sib_rs.at[0], sibling).wait_send()
        for k in range(NX):
            columns = pl.ds(pl.multiple_of((2 * k + 1 - c) * SLICE, 128), SLICE)
            sib_s[slot, k] = jnp.dot(block, down[:, columns], preferred_element_type=F32)
        remote(sib_s.at[slot], sib_r.at[b], sib_ss.at[slot], sib_rs.at[dz], sibling).start()
        for k in range(NX):
            columns = pl.ds(pl.multiple_of((2 * k + c) * SLICE, 128), SLICE)
            own[b, k] = jnp.dot(block, down[:, columns], preferred_element_type=F32)

    def x_scatter(dz):
        b = mod(z + dz, NZ)
        arrive(sib_r.at[b], sib_ss.at[0], sib_rs.at[dz])
        for j in (2, 1, 3):
            k = x3_parts[j]
            xs[b, j] = (own[b, k, :, 0:PW] + sib_r[b, k, :, 0:PW]).astype(BF16)
            push(xs.at[b, j], xr.at[b, j], x3_ss.at[dz, j], x3_rs.at[dz, j], at(x=k))

    def term(b, part):
        if part:
            k = part - 1
            return own[b, k, :, PW:] + sib_r[b, k, :, PW:]
        total = own[b, x, :, 0:PW] + sib_r[b, x, :, 0:PW]
        for j in range(1, NX):
            total += xr[b, j].astype(F32)
        return total

    def x_gathered(dz):
        b = mod(z + dz, NZ)
        for j in range(1, NX):
            arrive(xr.at[b, j], x3_ss.at[dz, j], x3_rs.at[dz, j])

    def far_parts(way):
        return (0, 3) if way == 0 else (3, 2)

    def chain_in(way, step):
        if step == 0:
            start, size = far_parts(way)
            arrive(zr.at[way, step, pl.ds(start, size)], z3_ss.at[way, step], z3_rs.at[way, step])
        else:
            arrive(zr.at[way, step], z3_ss.at[way, step], z3_rs.at[way, step])

    def chain(way, step):
        dz = 4 - step if way == 0 else 4 + step
        b = mod(z + dz, NZ)
        start, size = far_parts(way)
        if step:
            chain_in(way, step - 1)
        for part in range(5):
            received = start <= part < start + size
            if step == 0 and not received:
                continue
            total = term(b, part)
            if step > 1 or (step == 1 and received):
                total += zr[way, step - 1, part].astype(F32)
            zs[way, step, part] = total.astype(BF16)
        if step == 0:
            src, dst = zs.at[way, step, pl.ds(start, size)], zr.at[way, step, pl.ds(start, size)]
        else:
            src, dst = zs.at[way, step], zr.at[way, step]
        push(src, dst, z3_ss.at[way, step], z3_rs.at[way, step], step_to[way])

    down_block(4, 0)
    down_block(3, 1)
    x_scatter(4)
    down_block(5, 2)
    x_scatter(3)
    x_gathered(4)
    chain(0, 0)
    chain(1, 0)
    down_block(2, 3)
    x_scatter(5)
    down_block(6, 4)
    x_scatter(2)
    x_gathered(3)
    chain(0, 1)
    x_gathered(5)
    chain(1, 1)
    down_block(1, 5)
    x_scatter(6)
    down_block(7, 6)
    x_scatter(1)
    down_block(0, 7)
    x_scatter(7)
    x_gathered(2)
    chain(0, 2)
    x_gathered(6)
    chain(1, 2)
    x_scatter(0)
    x_gathered(1)
    chain(0, 3)
    x_gathered(7)
    chain(1, 3)
    x_gathered(0)
    chain_in(0, 3)
    chain_in(1, 3)

    def final(part):
        return term(z, part) + (zr[0, 3, part].astype(F32) + zr[1, 3, part].astype(F32))

    for k in range(NX):
        fxs[k] = final(1 + k).astype(BF16)
    for j in (2, 1, 3):
        k = x_peer[j]
        push(fxs.at[k], fxr.at[j], fx_ss.at[j], fx_rs.at[j], at(x=k))

    def y_send(half):
        for i in (2, 1, 3):
            span = pl.ds(pl.multiple_of(y_peer[i] * CAP, 8), CAP)
            push(ys.at[half, span], yr.at[half, y], y3_ss.at[half, i], y3_rs.at[half, i], at(y=y_peer[i]))
        yr[half, y] = ys[half, pl.ds(pl.multiple_of(y * CAP, 8), CAP)]

    ys[0] = final(0)
    y_send(0)
    total = own[z, x, :, PW:] + sib_r[z, x, :, PW:]
    total += zr[0, 3, 1 + x].astype(F32) + zr[1, 3, 1 + x].astype(F32)
    for j in range(1, NX):
        arrive(fxr.at[j], fx_ss.at[j], fx_rs.at[j])
        total += fxr[j].astype(F32)
    ys[1] = total
    y_send(1)
    for half in (0, 1):
        for i in range(1, NY):
            source = y_peer[NY - i]
            arrive(yr.at[half, source], y3_ss.at[half, i], y3_rs.at[half, i])
        for e in range(EXPERTS):
            out[e * CAP:(e + 1) * CAP, half * PW:(half + 1) * PW] = yr[half, e]
    for copy in sent:
        copy.wait_send()
    for slot in (0, 1):
        remote(sib_s.at[slot], sib_r.at[0], sib_ss.at[slot], sib_rs.at[0], sibling).wait_send()


def run(packed, gate_weight, up_weight, down_weight):
    vmem, dma = pltpu.VMEM, pltpu.SemaphoreType.DMA
    scratch = [
        vmem((D, UNITS), BF16), vmem((D, UNITS), BF16), vmem((UNITS, D), BF16),
        vmem((UNITS, UNITS), BF16),
        vmem((NY, TOK, 5 * PW), BF16),
        vmem((NZ, PARTS, BLK, PW), BF16),
        vmem((NZ, BLK, UNITS), F32), vmem((NZ, BLK, UNITS), F32),
        vmem((NZ, NX, 48, 128), BF16),
        vmem((NZ * NX, 48, 128), BF16), vmem((NZ * NX, 48, 128), BF16),
        vmem((NZ, NX, 48, 128), BF16),
        vmem((NZ, NX, BLK, SLICE), F32),
        vmem((2, NX, BLK, SLICE), F32),
        vmem((NZ, NX, BLK, SLICE), F32),
        vmem((NZ, NX, BLK, PW), BF16), vmem((NZ, NX, BLK, PW), BF16),
        vmem((2, 4, 5, BLK, PW), BF16), vmem((2, 4, 5, BLK, PW), BF16),
        vmem((NX, BLK, PW), BF16), vmem((NX, BLK, PW), BF16),
        vmem((2, BLK, PW), F32), vmem((2, NY, CAP, PW), F32),
        dma((3,)),
        dma((NY, 2)), dma((NY, 2)),
        dma((2, 5, 2)), dma((2, 5, 2)),
        dma((NZ, NX)), dma((NZ, NX)),
        dma((NZ, 5)), dma((NZ, 5)),
        dma((NZ,)), dma((NZ,)),
        dma((NZ, NX)), dma((1,)),
        dma((NZ, NX)), dma((NZ,)),
        dma((2,)), dma((NZ,)),
        dma((NZ, NX)), dma((NZ, NX)),
        dma((2, 4)), dma((2, 4)),
        dma((NX,)), dma((NX,)),
        dma((2, NY)), dma((2, NY)),
    ]
    return pl.pallas_call(
        kernel,
        out_shape=jax.ShapeDtypeStruct((BLK, SLICE), F32),
        in_specs=[pl.BlockSpec(memory_space=pltpu.VMEM)] + [pl.BlockSpec(memory_space=pl.ANY)] * 3,
        out_specs=pl.BlockSpec(memory_space=pltpu.VMEM),
        scratch_shapes=scratch,
        compiler_params=pltpu.CompilerParams(
            collective_id=1, has_side_effects=True, vmem_limit_bytes=63 * 2 ** 20
        ),
        name="experts",
    )(packed, gate_weight, up_weight, down_weight)


def on_device(tokens, expert_ids, router_logits, gate_weight, up_weight, down_weight):
    expert_range = jnp.arange(EXPERTS, dtype=jnp.int32)
    picked = expert_ids[:, :, None] == expert_range[None, None, :]
    chosen = jnp.any(picked, axis=1).astype(jnp.int32)
    slot_index = jnp.cumsum(chosen, axis=0) - chosen
    slot_range = jnp.arange(TOK, dtype=jnp.int32)
    placing = (chosen[:, :, None] == 1) & (slot_index[:, :, None] == slot_range[None, None, :])
    packed = jnp.einsum(
        "tem,td->emd", placing.astype(BF16), tokens, preferred_element_type=F32
    ).astype(BF16)
    returned = run(packed.reshape(EXPERTS * TOK, D), gate_weight, up_weight, down_weight)
    picked_logits = jnp.sum(jnp.where(picked, router_logits[:, None, :], 0.0), axis=2)
    first_share = 1.0 / (1.0 + jnp.exp(picked_logits[:, 1] - picked_logits[:, 0]))
    shares = jnp.stack([first_share, 1.0 - first_share], axis=1)
    weight_e = jnp.sum(jnp.where(picked, shares[:, :, None], 0.0), axis=1)
    combine = jnp.where(placing[:, :, :CAP], weight_e[:, :, None], 0.0).reshape(TOK, EXPERTS * CAP)
    output = lax.dot_general(
        combine, returned, (((1,), (0,)), ((), ())), precision=lax.Precision.HIGHEST
    )
    return output.astype(BF16)


def solution(mesh):
    placed = (
        P("ed", None),
        P("ed", None),
        P("ed", None),
        P("ed", None, "tp"),
        P("ed", None, "tp"),
        P("ed", "tp", None),
    )
    return jax.shard_map(
        on_device, mesh=mesh, in_specs=placed, out_specs=P("ed", "tp"), check_vma=False
    )
```

time: 573 us -> 141 us (0.25)
  waiting for transfers between devices: 282 us -> 0 us
  blocking collectives: 218 us -> 0 us
  Pallas kernels: 0 us -> 134 us
  starting transfers between devices: 22 us -> 0 us
  matrix products: 18.8 us -> 3.6 us
  between operations: 13.5 us -> 0.04 us
  other arithmetic: 14.6 us -> 2.29 us
    all_to_all x1 -> x0, blocking collectives: 218 us -> none  [on_device(): lax.all_to_all(outgoing, 'ed', split_axis=0, concat_axis=0, tiled=True)]
    pallas_call x0 -> x1, Pallas kernels: none -> 134 us  [run(): pl.pallas_call(kernel, out_shape=jax.ShapeDtypeStruct((BLK, SLICE), F32),...]
    ppermute x6 -> x0, waiting for transfers between devices: 126 us -> none  [from_partner(): return lax.ppermute(block, axis, route)]
    reduce_scatter x1 -> x0, waiting for transfers between devices: 102 us -> none  [on_device(): lax.psum_scatter(lax.dot_general(down_rows, rotated, (((0,), (1,)), ((),...]
    all_to_all x1 -> x0, waiting for transfers between devices: 53.4 us -> none  [on_device(): lax.all_to_all(partial_value, 'ed', split_axis=1, concat_axis=1, tiled=True)]
    dot_general x6 -> x2, matrix products: 18.8 us -> 3.6 us  [the longest x1 1.9 us: on_device(): lax.dot_general(combine, returned, (((1,), (0,)), ((), ())), precision=la...]
    ppermute x6 -> x0, starting transfers between devices: 11.8 us -> none  [from_partner(): return lax.ppermute(block, axis, route)]
    select_n x5 -> x1, other arithmetic: 11.8 us -> 0.01 us  [on_device(): jnp.where(placing[:, :, :CAP], weight_e[:, :, None], 0.0)]
  transfers between devices with their start and end apart: 8 -> 0, of which waited for: 8 -> 0; matrix products, arithmetic and copies ran while one was open for 0% -> 0% of each run, Pallas kernels for 0% -> 0%
where the time goes in v1:
time: 141 us; the launch traced here: 140 us
  Pallas kernels  134 us (95%)
  matrix products  3.6 us (3%)
  other arithmetic  2.29 us (2%)
    pallas_call x1, Pallas kernels, run(): pl.pallas_call(kernel, out_shape=jax.ShapeDtypeStruct((BLK, SLICE), F32),...  134 us

profile of v1, /device:TPU:8, one launch (start us, length us, event | category | flops | bytes accessed | tf_op | source)
XLA Modules:
  0.0 140.4 jit_solution(18445234479613780437)
XLA Ops:
  0.0 0.0 copy-start
  0.0 0.7 fusion.2
  0.7 0.7 select_reduce_fusion.1
  1.5 0.7 select_reduce_fusion
  2.2 0.1 copy.16
  2.3 0.1 copy.17
  2.4 0.1 reduce_window_sum.11
  2.5 0.1 copy.18
  2.6 0.0 copy-done
  2.6 1.7 %convolution_convert_fusion = bf16[4,32,6144]{2,1,0:T(8,128)(2,1)} fusion(bf16[32,6144]{1,0:T(8,128)(2,1)S(1)} %copy-done, s32[32,4]{0,1:T(4,128)S(1)} %copy.18, pred[32,4]{0,1:T(4,128)(4,1)S(1)} %copy.17), kind=kOutput, calls=%fused_computation | convolution fusion | flops 51126272 | bytes 1966720 | tf_op jit(solution)/shard_map/tem,td->emd/dot_general | solution.py:456
  4.3 134.2 %experts.1 = f32[96,768]{1,0:T(8,128)} custom-call(bf16[128,6144]{1,0:T(8,128)(2,1)} %bitcast.7, bf16[1,6144,256]{2,1,0:T(8,128)(2,1)} %gate_hbm.1, bf16[1,6144,256]{2,1,0:T(8,128)(2,1)} %up_hbm.1, bf16[1,256,6144]{2,1,0:T(8,128)(2,1)} %down_hbm.1), custom_call_target="tpu_custom_call" | custom-call | tf_op jit(solution)/shard_map/experts/pallas_call | solution.py:436
  138.5 1.9 %convolution_convert_fusion.1 = bf16[32,768]{1,0:T(8,128)(2,1)} fusion(f32[32,96]{0,1:T(8,128)S(1)} %bitcast.8, f32[96,768]{1,0:T(8,128)} %experts.1), kind=kOutput, calls=%fused_computation.1 | convolution fusion | flops 28336128 | bytes 356352 | tf_op jit(solution)/shard_map/dot_general | solution.py:465
  (6 shorter events, 0.1 us)
Async XLA Ops:
  0.0 2.6 %copy-start = (bf16[32,6144]{1,0:T(8,128)(2,1)S(1)}, bf16[32,6144]{1,0:T(8,128)(2,1)}, u32[]{:S(2)}) copy-start(bf16[32,6144]{1,0:T(8,128)(2,1)} %param.6) | copy-start | bytes 1179652

commit v2 on v1

v2 whole, which is shorter than its diff:
```python
import jax
import jax.numpy as jnp
from jax import lax
from jax.experimental import pallas as pl
from jax.experimental.pallas import tpu as pltpu
from jax.sharding import PartitionSpec as P

MESH = pl.DeviceIdType.MESH
BF16, F32 = jnp.bfloat16, jnp.float32
D = 6144
FF = 16384
EXPERTS = 4
TOK = 32
CAP = 24
NX, NY, NZ = 4, 4, 8
BLK = EXPERTS * CAP
PW = 384
PARTS = D // PW
UNITS = 256
SLICE = 768
HALF = PARTS // 2


def mod(value, count):
    return lax.rem(value + count, count)


def kernel(
    tokens_hbm, expert_ids, router_logits, gate_hbm, up_hbm, down_hbm, out,
    tokens, packed, gate, up, down, had, ybuf, rows, core_s, core_r, a2a_s, a2a_r, wide_r, back_s, rot,
    own, sib_s, sib_r, xs, xr, zs, zr, fxs, fxr, ys, yr,
    t_sem, w_sem, y_ss, y_rs, z_ss, z_rs, x_ss, x_rs, s_ss, s_rs, c_ss, c_rs, a_ss, a_rs, b_ss, b_rs,
    sib_ss, sib_rs, x3_ss, x3_rs, z3_ss, z3_rs, fx_ss, fx_rs, y3_ss, y3_rs,
):
    ed, tp = lax.axis_index("ed"), lax.axis_index("tp")
    y, z = lax.div(ed, NZ), lax.rem(ed, NZ)
    x, c = lax.div(tp, 2), lax.rem(tp, 2)

    def at(x=x, y=y, z=z, c=c):
        return (y * NZ + z, x * 2 + c)

    sibling = at(c=1 - c)
    x_peer = [mod(x + i, NX) for i in range(NX)]
    y_peer = [mod(y + i, NY) for i in range(NY)]
    step_to = (at(z=mod(z + 1, NZ)), at(z=mod(z - 1, NZ)))

    def remote(src, dst, send, recv, device):
        return pltpu.make_async_remote_copy(
            src_ref=src, dst_ref=dst, send_sem=send, recv_sem=recv, device_id=device, device_id_type=MESH
        )

    sent = []

    def push(src, dst, send, recv, device):
        copy = remote(src, dst, send, recv, device)
        copy.start()
        sent.append(copy)

    def arrive(dst, send, recv):
        remote(dst, dst, send, recv, sibling).wait_recv()

    tokens_copy = pltpu.make_async_copy(tokens_hbm, tokens, t_sem)
    tokens_copy.start()
    weights = [
        pltpu.make_async_copy(gate_hbm.at[0], gate, w_sem.at[0]),
        pltpu.make_async_copy(up_hbm.at[0], up, w_sem.at[1]),
        pltpu.make_async_copy(down_hbm.at[0], down, w_sem.at[2]),
    ]
    for copy in weights:
        copy.start()

    barrier = pltpu.get_barrier_semaphore()
    greeted = [sibling, *step_to]
    greeted += [at(x=x_peer[i]) for i in range(1, NX)]
    greeted += [at(y=y_peer[i]) for i in range(1, NY)]
    for device in greeted:
        pl.semaphore_signal(barrier, inc=1, device_id=device, device_id_type=MESH)
    pl.semaphore_wait(barrier, len(greeted))

    tok_row = lax.broadcasted_iota(jnp.int32, (TOK, TOK), 0)
    tok_col = lax.broadcasted_iota(jnp.int32, (TOK, TOK), 1)
    before = (tok_row > tok_col).astype(F32).astype(BF16)

    def column(values):
        return jnp.sum(jnp.where(tok_row == tok_col, values, jnp.zeros_like(values)), axis=1, keepdims=True)

    first, second = column(expert_ids[0:1, :]), column(expert_ids[1:2, :])

    def place(capacity):
        lane = lax.broadcasted_iota(jnp.int32, (TOK, EXPERTS * capacity), 1)
        expert = jnp.zeros_like(lane)
        for e in range(1, EXPERTS):
            expert += (lane >= e * capacity).astype(jnp.int32)
        chosen = (first == expert) | (second == expert)
        count = jnp.dot(before, chosen.astype(F32).astype(BF16), preferred_element_type=F32)
        return expert, chosen & (count == (lane - expert * capacity).astype(F32))

    _, placing = place(TOK)
    placing = placing.astype(F32).astype(BF16)

    base = c * HALF
    wide, narrow = 4 * PW, PW
    shared = base + 4 + x
    cols_wide = pl.ds(pl.multiple_of(base * PW, 128), wide)
    cols_narrow = pl.ds(pl.multiple_of(shared * PW, 128), narrow)
    tokens_copy.wait()
    for kind, columns, span in ((0, cols_narrow, pl.ds(wide, narrow)), (1, cols_wide, pl.ds(0, wide))):
        packed[:, span] = lax.dot_general(
            placing, tokens[:, columns], (((0,), (0,)), ((), ())), preferred_element_type=F32
        ).astype(BF16)
        for i in (2, 1, 3):
            slot = pl.ds(pl.multiple_of(y_peer[i] * TOK, TOK), TOK)
            push(packed.at[slot, span], ybuf.at[y, :, span], y_ss.at[i, kind], y_rs.at[i, kind], at(y=y_peer[i]))
    ybuf[y] = packed[pl.ds(pl.multiple_of(y * TOK, TOK), TOK), :]

    both = lax.broadcasted_iota(jnp.int32, (UNITS, UNITS), 0) & lax.broadcasted_iota(jnp.int32, (UNITS, UNITS), 1)
    for shift in (4, 2, 1):
        both = both ^ (both >> shift)
    had[...] = (1 - 2 * (both & 1)).astype(F32).astype(BF16)

    i_row = lax.broadcasted_iota(jnp.int32, (BLK, NY * TOK), 0)
    i_col = lax.broadcasted_iota(jnp.int32, (BLK, NY * TOK), 1)
    squeeze = jnp.zeros((BLK, NY * TOK), F32)
    for s in range(NY):
        inside = (i_row >= CAP * s) & (i_row < CAP * (s + 1)) & (i_col - TOK * s == i_row - CAP * s)
        squeeze = jnp.where(inside, 1.0, squeeze)
    squeeze = squeeze.astype(BF16)

    blocks = [z]
    for t in (1, 2, 3):
        blocks += [mod(z - t, NZ), mod(z + t, NZ)]
    blocks.append(mod(z + 4, NZ))

    def parts_of(b, g):
        return rows.at[b, shared] if g == 0 else rows.at[b, pl.ds(base + 2 * (g - 1), 2)]

    def goes(way, t, g):
        return t < 4 or (g < 2) == (way == 0)

    def z_send(b, way, t, g):
        if t <= 4 and goes(way, t, g):
            part = parts_of(b, g)
            push(part, part, z_ss.at[way, t, g], z_rs.at[way, t, g], step_to[way])

    def share(b, i, g):
        part = parts_of(b, g)
        if g == 0:
            for j in (2, 1, 3):
                push(part, part, x_ss.at[i, j], x_rs.at[i, j], at(x=x_peer[j]))
        push(part, part, s_ss.at[i, 3 + g], s_rs.at[i, 3 + g], sibling)

    def x_pass(b, i):
        for j in (1, 3, 2):
            part = rows.at[b, base + 4 + x_peer[NX - j]]
            arrive(part, x_ss.at[i, j], x_rs.at[i, j])
            push(part, part, s_ss.at[i, j - 1], s_rs.at[i, j - 1], sibling)

    other = (1 - c) * HALF

    def ready(b, i):
        arrive(rows.at[b, other + 4 + x], s_ss.at[i, 3], s_rs.at[i, 3])
        for g in (1, 2):
            arrive(rows.at[b, pl.ds(other + 2 * (g - 1), 2)], s_ss.at[i, 3 + g], s_rs.at[i, 3 + g])
        for j in range(1, NX):
            part = rows.at[b, other + 4 + x_peer[NX - j]]
            arrive(part, s_ss.at[i, j - 1], s_rs.at[i, j - 1])

    def hidden(b):
        gate_act = jnp.zeros((BLK, UNITS), F32)
        up_act = jnp.zeros((BLK, UNITS), F32)
        for p in range(0, PARTS, 2):
            block = jnp.concatenate([rows[b, p], rows[b, p + 1]], axis=1)
            gate_act += jnp.dot(block, gate[p * PW:(p + 2) * PW, :], preferred_element_type=F32)
            up_act += jnp.dot(block, up[p * PW:(p + 2) * PW, :], preferred_element_type=F32)
        value = gate_act / (1.0 + jnp.exp(-gate_act)) * up_act
        high = value.astype(BF16)
        low = (value - high.astype(F32)).astype(BF16)
        core_s[b] = jnp.dot(high, had[...], preferred_element_type=F32) + jnp.dot(
            low, had[...], preferred_element_type=F32
        )

    def core_push(b, i):
        push(core_s.at[b], core_r.at[b], c_ss.at[i], c_rs.at[i], sibling)

    sign = (1 - 2 * c).astype(F32)
    me32 = z * NX + x

    def spread(b, i):
        arrive(core_r.at[b], c_ss.at[i], c_rs.at[i])
        value = (core_r[b] + sign * core_s[b]).astype(BF16)
        for k in range(NX):
            a2a_s[b, k] = value[48 * (k // 2):48 * (k // 2) + 48, 128 * (k % 2):128 * (k % 2) + 128]
        for j in range(NX):
            k = x_peer[j]
            if i == 0 and j == 0:
                a2a_r[me32] = a2a_s[b, k]
            else:
                push(a2a_s.at[b, k], a2a_r.at[me32], a_ss.at[i, j], a_rs.at[0], at(x=k, z=b))

    def squeezed(at_col):
        block = ybuf[:, :, at_col:at_col + PW].reshape(NY * TOK, PW)
        return jnp.dot(squeeze, block, preferred_element_type=F32).astype(BF16)

    ahead = []
    for g in (0, 1, 2):
        if g < 2:
            span = pl.ds(wide, narrow) if g == 0 else pl.ds(0, wide)
            for i in range(1, NY):
                arrive(ybuf.at[y_peer[NY - i], :, span], y_ss.at[i, g], y_rs.at[i, g])
        if g == 0:
            rows[z, shared] = squeezed(wide)
        else:
            for p in (2 * g - 2, 2 * g - 1):
                rows[z, base + p] = squeezed(p * PW)
        if g == 2:
            for copy in ahead:
                copy.wait_send()
        for way in (0, 1):
            z_send(z, way, 1, g)
            ahead.append(sent.pop())
        share(z, 0, g)

    sent.extend(ahead[4:])
    for copy in weights[:2]:
        copy.wait()

    def group(t):
        if t == 0:
            return [0]
        return [2 * t - 1, 2 * t] if t < 4 else [7]

    def work(i):
        ready(blocks[i], i)
        hidden(blocks[i])
        core_push(blocks[i], i)

    for t in (1, 2, 3, 4):
        for g in (0, 1, 2):
            for way in (0, 1):
                if not goes(way, t, g):
                    continue
                i = group(t)[way] if t < 4 else 7
                b = blocks[i]
                arrive(parts_of(b, g), z_ss.at[way, t, g], z_rs.at[way, t, g])
                z_send(b, way, t + 1, g)
                share(b, i, g)
            if g == 0 and t >= 2:
                for i in group(t - 2):
                    spread(blocks[i], i)
            if g == 1:
                for i in group(t - 1):
                    x_pass(blocks[i], i)
            if 0 < g <= len(group(t - 1)):
                work(group(t - 1)[g - 1])
    x_pass(blocks[7], 7)
    for i in group(3):
        spread(blocks[i], i)
    work(7)
    spread(blocks[7], 7)

    remote(a2a_r.at[pl.ds(0, 31)], a2a_r.at[pl.ds(0, 31)], a_ss.at[0, 0], a_rs.at[0], sibling).wait_recv()
    count = NZ * NX

    def butterfly(values):
        stride = 1
        while stride < len(values):
            for low in range(len(values)):
                if low & stride == 0:
                    upper, lower = values[low], values[low + stride]
                    values[low], values[low + stride] = upper + lower, upper - lower
            stride *= 2
        return values

    for r in range(0, 48, 16):
        for s in range(0, count, 8):
            values = butterfly([a2a_r[s + n, r:r + 16, :].astype(F32) for n in range(8)])
            for n in range(8):
                wide_r[s + n, r:r + 16, :] = values[n]
        for n in range(8):
            values = butterfly([wide_r[n + 8 * q, r:r + 16, :] for q in range(4)])
            for q in range(4):
                back_s[n + 8 * q, r:r + 16, :] = (values[q] * FF ** -0.5).astype(BF16)

    rot[z, x] = back_s[me32]
    for dz in (4, 3, 5, 2, 6, 1, 7, 0):
        zz = mod(z + dz, NZ)
        for j in range(NX):
            if dz + j:
                s = zz * NX + x_peer[j]
                push(back_s.at[s], rot.at[z, x], b_ss.at[dz, j], b_rs.at[z], at(x=x_peer[j], z=zz))

    weights[2].wait()
    order = [4, 3, 5, 2, 6, 1, 7, 0]
    x3_parts = [mod(x + i, NX) for i in range(NX)]

    def down_block(dz, turn):
        b = mod(z + dz, NZ)
        if dz:
            arrive(rot.at[b], b_ss.at[0, 1], b_rs.at[b])
        else:
            arrive(rot.at[b, pl.ds(0, 3)], b_ss.at[0, 1], b_rs.at[b])
        upper = jnp.concatenate([rot[b, 0], rot[b, 1]], axis=1)
        lower = jnp.concatenate([rot[b, 2], rot[b, 3]], axis=1)
        block = jnp.concatenate([upper, lower], axis=0)
        slot = turn % 2
        if turn >= 2:
            remote(sib_s.at[slot], sib_r.at[b], sib_ss.at[slot], sib_rs.at[0], sibling).wait_send()
        for k in range(NX):
            columns = pl.ds(pl.multiple_of((2 * k + 1 - c) * SLICE, 128), SLICE)
            sib_s[slot, k] = jnp.dot(block, down[:, columns], preferred_element_type=F32)
        remote(sib_s.at[slot], sib_r.at[b], sib_ss.at[slot], sib_rs.at[dz], sibling).start()
        for k in range(NX):
            columns = pl.ds(pl.multiple_of((2 * k + c) * SLICE, 128), SLICE)
            own[b, k] = jnp.dot(block, down[:, columns], preferred_element_type=F32)

    def x_scatter(dz):
        b = mod(z + dz, NZ)
        arrive(sib_r.at[b], sib_ss.at[0], sib_rs.at[dz])
        for j in (2, 1, 3):
            k = x3_parts[j]
            xs[b, j] = (own[b, k, :, 0:PW] + sib_r[b, k, :, 0:PW]).astype(BF16)
            push(xs.at[b, j], xr.at[b, j], x3_ss.at[dz, j], x3_rs.at[dz, j], at(x=k))

    def term(b, part):
        if part:
            k = part - 1
            return own[b, k, :, PW:] + sib_r[b, k, :, PW:]
        total = own[b, x, :, 0:PW] + sib_r[b, x, :, 0:PW]
        for j in range(1, NX):
            total += xr[b, j].astype(F32)
        return total

    def x_gathered(dz):
        b = mod(z + dz, NZ)
        for j in range(1, NX):
            arrive(xr.at[b, j], x3_ss.at[dz, j], x3_rs.at[dz, j])

    def far(way, part):
        return (part < 3) == (way == 0)

    def chain_in(way, step, part):
        arrive(zr.at[way, step, part], z3_ss.at[way, step, part], z3_rs.at[way, step, part])

    def chain(step, parts):
        for part in parts:
            for way in (0, 1):
                if step == 0 and not far(way, part):
                    continue
                total = term(mod(z + (4 - step if way == 0 else 4 + step), NZ), part)
                if step > 1 or (step == 1 and far(way, part)):
                    chain_in(way, step - 1, part)
                    total += zr[way, step - 1, part].astype(F32)
                zs[way, step, part] = total.astype(BF16)
                push(
                    zs.at[way, step, part], zr.at[way, step, part],
                    z3_ss.at[way, step, part], z3_rs.at[way, step, part], step_to[way],
                )

    down_block(4, 0)
    down_block(3, 1)
    x_scatter(4)
    chain(0, (1, 3, 2, 4))
    down_block(5, 2)
    x_scatter(3)
    down_block(2, 3)
    x_scatter(5)
    x_gathered(4)
    chain(0, (0,))
    chain(1, (1, 2, 3, 4))
    down_block(6, 4)
    x_scatter(2)
    down_block(1, 5)
    x_gathered(3)
    x_gathered(5)
    chain(1, (0,))
    x_scatter(6)
    chain(2, (1, 2, 3, 4))
    down_block(7, 6)
    x_scatter(1)
    down_block(0, 7)
    x_gathered(2)
    x_gathered(6)
    chain(2, (0,))
    x_scatter(7)
    chain(3, (1, 2, 3, 4))
    x_scatter(0)
    x_gathered(1)
    x_gathered(7)
    chain(3, (0,))
    x_gathered(0)

    def final(part):
        return term(z, part) + (zr[0, 3, part].astype(F32) + zr[1, 3, part].astype(F32))

    for k in range(NX):
        for way in (0, 1):
            chain_in(way, 3, 1 + k)
        fxs[k] = final(1 + k).astype(BF16)
    for j in (2, 1, 3):
        k = x_peer[j]
        push(fxs.at[k], fxr.at[j], fx_ss.at[j], fx_rs.at[j], at(x=k))

    def y_send(half):
        for i in (2, 1, 3):
            span = pl.ds(pl.multiple_of(y_peer[i] * CAP, 8), CAP)
            push(ys.at[half, span], yr.at[half, y], y3_ss.at[half, i], y3_rs.at[half, i], at(y=y_peer[i]))
        yr[half, y] = ys[half, pl.ds(pl.multiple_of(y * CAP, 8), CAP)]

    for way in (0, 1):
        chain_in(way, 3, 0)
    ys[0] = final(0)
    y_send(0)
    total = own[z, x, :, PW:] + sib_r[z, x, :, PW:]
    total += zr[0, 3, 1 + x].astype(F32) + zr[1, 3, 1 + x].astype(F32)

    logits = [column(router_logits[e:e + 1, :]) for e in range(EXPERTS)]
    picked = []
    for ids in (first, second):
        value = logits[0]
        for e in range(1, EXPERTS):
            value = jnp.where(ids == e, logits[e], value)
        picked.append(value)
    share0 = 1.0 / (1.0 + jnp.exp(picked[1] - picked[0]))
    expert, placed = place(CAP)
    combine = jnp.where(placed, jnp.where(first == expert, share0, 1.0 - share0), 0.0)

    for j in range(1, NX):
        arrive(fxr.at[j], fx_ss.at[j], fx_rs.at[j])
        total += fxr[j].astype(F32)
    ys[1] = total
    y_send(1)
    for half in (0, 1):
        for i in range(1, NY):
            source = y_peer[NY - i]
            arrive(yr.at[half, source], y3_ss.at[half, i], y3_rs.at[half, i])
        out[:, half * PW:(half + 1) * PW] = jnp.dot(
            combine, yr[half].reshape(EXPERTS * CAP, PW), precision=lax.Precision.HIGHEST, preferred_element_type=F32
        ).astype(BF16)
    for copy in sent:
        copy.wait_send()
    for slot in (0, 1):
        remote(sib_s.at[slot], sib_r.at[0], sib_ss.at[slot], sib_rs.at[0], sibling).wait_send()


def run(tokens, expert_ids, router_logits, gate_weight, up_weight, down_weight):
    vmem, dma = pltpu.VMEM, pltpu.SemaphoreType.DMA
    scratch = [
        vmem((TOK, D), BF16), vmem((EXPERTS * TOK, 5 * PW), BF16),
        vmem((D, UNITS), BF16), vmem((D, UNITS), BF16), vmem((UNITS, D), BF16),
        vmem((UNITS, UNITS), BF16),
        vmem((NY, TOK, 5 * PW), BF16),
        vmem((NZ, PARTS, BLK, PW), BF16),
        vmem((NZ, BLK, UNITS), F32), vmem((NZ, BLK, UNITS), F32),
        vmem((NZ, NX, 48, 128), BF16),
        vmem((NZ * NX, 48, 128), BF16),
        vmem((NZ * NX, 48, 128), F32), vmem((NZ * NX, 48, 128), BF16),
        vmem((NZ, NX, 48, 128), BF16),
        vmem((NZ, NX, BLK, SLICE), F32),
        vmem((2, NX, BLK, SLICE), F32),
        vmem((NZ, NX, BLK, SLICE), F32),
        vmem((NZ, NX, BLK, PW), BF16), vmem((NZ, NX, BLK, PW), BF16),
        vmem((2, 4, 5, BLK, PW), BF16), vmem((2, 4, 5, BLK, PW), BF16),
        vmem((NX, BLK, PW), BF16), vmem((NX, BLK, PW), BF16),
        vmem((2, BLK, PW), F32), vmem((2, NY, CAP, PW), F32),
        dma, dma((3,)),
        dma((NY, 2)), dma((NY, 2)),
        dma((2, 5, 3)), dma((2, 5, 3)),
        dma((NZ, NX)), dma((NZ, NX)),
        dma((NZ, 6)), dma((NZ, 6)),
        dma((NZ,)), dma((NZ,)),
        dma((NZ, NX)), dma((1,)),
        dma((NZ, NX)), dma((NZ,)),
        dma((2,)), dma((NZ,)),
        dma((NZ, NX)), dma((NZ, NX)),
        dma((2, 4, 5)), dma((2, 4, 5)),
        dma((NX,)), dma((NX,)),
        dma((2, NY)), dma((2, NY)),
    ]
    return pl.pallas_call(
        kernel,
        out_shape=jax.ShapeDtypeStruct((TOK, SLICE), BF16),
        in_specs=[pl.BlockSpec(memory_space=pl.ANY)]
        + [pl.BlockSpec(memory_space=pltpu.VMEM)] * 2
        + [pl.BlockSpec(memory_space=pl.ANY)] * 3,
        out_specs=pl.BlockSpec(memory_space=pltpu.VMEM),
        scratch_shapes=scratch,
        compiler_params=pltpu.CompilerParams(
            collective_id=1, has_side_effects=True, vmem_limit_bytes=63 * 2 ** 20
        ),
        name="experts",
    )(tokens, expert_ids.T, router_logits.T, gate_weight, up_weight, down_weight)


def solution(mesh):
    placed = (
        P("ed", None),
        P("ed", None),
        P("ed", None),
        P("ed", None, "tp"),
        P("ed", None, "tp"),
        P("ed", "tp", None),
    )
    return jax.shard_map(
        run, mesh=mesh, in_specs=placed, out_specs=P("ed", "tp"), check_vma=False
    )
```

time: 141 us -> 122 us (0.87); the launches traced: 140 us -> 120 us
  Pallas kernels: 134 us -> 119 us
  matrix products: 3.6 us -> 0 us
  other arithmetic: 2.29 us -> 0 us
    pallas_call x1, Pallas kernels: 134 us -> 119 us  [run(): pl.pallas_call(kernel, out_shape=jax.ShapeDtypeStruct((TOK, SLICE), BF16)...]
    dot_general x2 -> x0, matrix products: 3.6 us -> none  [the longest x1 1.9 us: on_device(): lax.dot_general(combine, returned, (((1,), (0,)), ((), ())), precision=la...]
    unnamed x2 -> x1, local copies, waits for them, and re-layouts: 0.01 us -> 1.42 us
    reduce_sum x2 -> x0, other arithmetic: 1.41 us -> none  [the longest x1 0.71 us: on_device(): jnp.sum(jnp.where(picked, router_logits[:, None, :], 0.0), axis=2)]
where the time goes in v2:
time: 122 us; the launch traced here: 120 us
  Pallas kernels  119 us (98%)
  local copies, waits for them, and re-layouts  1.42 us (1%)
    pallas_call x1, Pallas kernels, run(): pl.pallas_call(kernel, out_shape=jax.ShapeDtypeStruct((TOK, SLICE), BF16)...  119 us

profile of v2, /device:TPU:8, one launch (start us, length us, event | category | flops | bytes accessed | tf_op | source)
XLA Modules:
  0.0 119.9 jit_solution(13904970281643341213)
XLA Ops:
  0.0 118.5 %experts.1 = bf16[32,768]{1,0:T(8,128)(2,1)} custom-call(bf16[32,6144]{1,0:T(8,128)(2,1)} %tokens_hbm.1, s32[2,32]{1,0:T(2,128)} %bitcast.3, f32[4,32]{1,0:T(4,128)} %bitcast.2, bf16[1,6144,256]{2,1,0:T(8,128)(2,1)} %gate_hbm.1, bf16[1,6144,256]{2,1,0:T(8,128)(2,1)} %up_hbm.1, bf16[1,256,6144]{2,1,0:T(8,128)(2,1)} %down_hbm.1), custom_call_target="tpu_custom_call" | custom-call | tf_op jit(solution)/shard_map/experts/pallas_call | solution.py:479
  118.5 1.4 %copy.8 = bf16[32,768]{1,0:T(8,128)(2,1)} copy(bf16[32,768]{1,0:T(8,128)(2,1)} %experts.1) | data formatting | bytes 98304

commit v3 on v2

--- a/solution.py
+++ b/solution.py
@@ -14,11 +14,13 @@
 CAP = 24
 NX, NY, NZ = 4, 4, 8
 BLK = EXPERTS * CAP
-PW = 384
+PW = 512
 PARTS = D // PW
 UNITS = 256
 SLICE = 768
 HALF = PARTS // 2
+HB = BLK // 2
+ZW = SLICE - PW
 
 
 def mod(value, count):
@@ -28,7 +30,7 @@
 def kernel(
     tokens_hbm, expert_ids, router_logits, gate_hbm, up_hbm, down_hbm, out,
     tokens, packed, gate, up, down, had, ybuf, rows, core_s, core_r, a2a_s, a2a_r, wide_r, back_s, rot,
-    own, sib_s, sib_r, xs, xr, zs, zr, fxs, fxr, ys, yr,
+    own, sib_s, sib_r, xs, xr, zs, zr, fxf, fxs, fxr, ysa, ysb, yra, yrb,
     t_sem, w_sem, y_ss, y_rs, z_ss, z_rs, x_ss, x_rs, s_ss, s_rs, c_ss, c_rs, a_ss, a_rs, b_ss, b_rs,
     sib_ss, sib_rs, x3_ss, x3_rs, z3_ss, z3_rs, fx_ss, fx_rs, y3_ss, y3_rs,
 ):
@@ -73,9 +75,9 @@
     greeted = [sibling, *step_to]
     greeted += [at(x=x_peer[i]) for i in range(1, NX)]
     greeted += [at(y=y_peer[i]) for i in range(1, NY)]
+    greeted += [at(x=x_peer[i], z=mod(z + dz, NZ)) for dz in (3, 4, 5) for i in range(NX)]
     for device in greeted:
         pl.semaphore_signal(barrier, inc=1, device_id=device, device_id_type=MESH)
-    pl.semaphore_wait(barrier, len(greeted))
 
     tok_row = lax.broadcasted_iota(jnp.int32, (TOK, TOK), 0)
     tok_col = lax.broadcasted_iota(jnp.int32, (TOK, TOK), 1)
@@ -99,15 +101,18 @@
     placing = placing.astype(F32).astype(BF16)
 
     base = c * HALF
-    wide, narrow = 4 * PW, PW
-    shared = base + 4 + x
+    wide, narrow = 2 * PW, PW
+    shared = base + 2 + x
     cols_wide = pl.ds(pl.multiple_of(base * PW, 128), wide)
     cols_narrow = pl.ds(pl.multiple_of(shared * PW, 128), narrow)
     tokens_copy.wait()
-    for kind, columns, span in ((0, cols_narrow, pl.ds(wide, narrow)), (1, cols_wide, pl.ds(0, wide))):
+    kinds = ((0, cols_narrow, pl.ds(wide, narrow)), (1, cols_wide, pl.ds(0, wide)))
+    for _, columns, span in kinds:
         packed[:, span] = lax.dot_general(
             placing, tokens[:, columns], (((0,), (0,)), ((), ())), preferred_element_type=F32
         ).astype(BF16)
+    pl.semaphore_wait(barrier, len(greeted))
+    for kind, _, span in kinds:
         for i in (2, 1, 3):
             slot = pl.ds(pl.multiple_of(y_peer[i] * TOK, TOK), TOK)
             push(packed.at[slot, span], ybuf.at[y, :, span], y_ss.at[i, kind], y_rs.at[i, kind], at(y=y_peer[i]))
@@ -131,53 +136,74 @@
         blocks += [mod(z - t, NZ), mod(z + t, NZ)]
     blocks.append(mod(z + 4, NZ))
 
-    def parts_of(b, g):
-        return rows.at[b, shared] if g == 0 else rows.at[b, pl.ds(base + 2 * (g - 1), 2)]
+    def part_of(b, g):
+        return rows.at[b, shared if g == 0 else base + g - 1]
+
+    def z_part(b, way, t, g):
+        if t == 4 and g == 1:
+            return rows.at[b, base, pl.ds(HB * way, HB)]
+        return part_of(b, g)
 
     def goes(way, t, g):
-        return t < 4 or (g < 2) == (way == 0)
+        return t < 4 or g == 1 or (g == 0) == (way == 0)
 
     def z_send(b, way, t, g):
         if t <= 4 and goes(way, t, g):
-            part = parts_of(b, g)
+            part = z_part(b, way, t, g)
             push(part, part, z_ss.at[way, t, g], z_rs.at[way, t, g], step_to[way])
 
     def share(b, i, g):
-        part = parts_of(b, g)
+        part = part_of(b, g)
         if g == 0:
-            for j in (2, 1, 3):
+            for j in (2, 1, 3) if i == 7 else (1, 3):
                 push(part, part, x_ss.at[i, j], x_rs.at[i, j], at(x=x_peer[j]))
         push(part, part, s_ss.at[i, 3 + g], s_rs.at[i, 3 + g], sibling)
 
-    def x_pass(b, i):
-        for j in (1, 3, 2):
-            part = rows.at[b, base + 4 + x_peer[NX - j]]
+    def x_near(b, i):
+        for j in (1, 3):
+            index = base + 2 + x_peer[NX - j]
+            part = rows.at[b, index]
             arrive(part, x_ss.at[i, j], x_rs.at[i, j])
+            if i < 7:
+                half = rows.at[b, index, pl.ds(HB * (j // 2), HB)]
+                push(half, half, x_ss.at[i, 2 - 2 * (j // 2)], x_rs.at[i, 2 - 2 * (j // 2)], at(x=x_peer[j]))
             push(part, part, s_ss.at[i, j - 1], s_rs.at[i, j - 1], sibling)
 
+    def x_far(b, i):
+        index = base + 2 + x_peer[2]
+        part = rows.at[b, index]
+        if i < 7:
+            for h in (0, 1):
+                arrive(rows.at[b, index, pl.ds(HB * h, HB)], x_ss.at[i, 2 - 2 * h], x_rs.at[i, 2 - 2 * h])
+        else:
+            arrive(part, x_ss.at[i, 2], x_rs.at[i, 2])
+        push(part, part, s_ss.at[i, 1], s_rs.at[i, 1], sibling)
+
     other = (1 - c) * HALF
 
     def ready(b, i):
-        arrive(rows.at[b, other + 4 + x], s_ss.at[i, 3], s_rs.at[i, 3])
-        for g in (1, 2):
-            arrive(rows.at[b, pl.ds(other + 2 * (g - 1), 2)], s_ss.at[i, 3 + g], s_rs.at[i, 3 + g])
+        for g in range(3):
+            arrive(rows.at[b, other + 2 + x if g == 0 else other + g - 1], s_ss.at[i, 3 + g], s_rs.at[i, 3 + g])
         for j in range(1, NX):
-            part = rows.at[b, other + 4 + x_peer[NX - j]]
-            arrive(part, s_ss.at[i, j - 1], s_rs.at[i, j - 1])
-
-    def hidden(b):
-        gate_act = jnp.zeros((BLK, UNITS), F32)
-        up_act = jnp.zeros((BLK, UNITS), F32)
-        for p in range(0, PARTS, 2):
-            block = jnp.concatenate([rows[b, p], rows[b, p + 1]], axis=1)
-            gate_act += jnp.dot(block, gate[p * PW:(p + 2) * PW, :], preferred_element_type=F32)
-            up_act += jnp.dot(block, up[p * PW:(p + 2) * PW, :], preferred_element_type=F32)
+            arrive(rows.at[b, other + 2 + x_peer[NX - j]], s_ss.at[i, j - 1], s_rs.at[i, j - 1])
+
+    def hidden(group):
+        gate_act = jnp.zeros((BLK * len(group), UNITS), F32)
+        up_act = jnp.zeros((BLK * len(group), UNITS), F32)
+        for p in range(PARTS):
+            span = slice(p * PW, (p + 1) * PW)
+            pieces = [rows[blocks[i], p] for i in group]
+            block = pieces[0] if len(pieces) == 1 else jnp.concatenate(pieces, axis=0)
+            gate_act += jnp.dot(block, gate[span, :], preferred_element_type=F32)
+            up_act += jnp.dot(block, up[span, :], preferred_element_type=F32)
         value = gate_act / (1.0 + jnp.exp(-gate_act)) * up_act
         high = value.astype(BF16)
         low = (value - high.astype(F32)).astype(BF16)
-        core_s[b] = jnp.dot(high, had[...], preferred_element_type=F32) + jnp.dot(
+        turned = jnp.dot(high, had[...], preferred_element_type=F32) + jnp.dot(
             low, had[...], preferred_element_type=F32
         )
+        for n, i in enumerate(group):
+            core_s[blocks[i]] = turned[BLK * n:BLK * n + BLK]
 
     def core_push(b, i):
         push(core_s.at[b], core_r.at[b], c_ss.at[i], c_rs.at[i], sibling)
@@ -192,16 +218,15 @@
             a2a_s[b, k] = value[48 * (k // 2):48 * (k // 2) + 48, 128 * (k % 2):128 * (k % 2) + 128]
         for j in range(NX):
             k = x_peer[j]
-            if i == 0 and j == 0:
+            if i == 7 and j == 0:
                 a2a_r[me32] = a2a_s[b, k]
             else:
-                push(a2a_s.at[b, k], a2a_r.at[me32], a_ss.at[i, j], a_rs.at[0], at(x=k, z=b))
+                push(a2a_s.at[b, k], a2a_r.at[me32], a_ss.at[i, j], a_rs.at[0], at(x=k, z=mod(b + 4, NZ)))
 
     def squeezed(at_col):
         block = ybuf[:, :, at_col:at_col + PW].reshape(NY * TOK, PW)
         return jnp.dot(squeeze, block, preferred_element_type=F32).astype(BF16)
 
-    ahead = []
     for g in (0, 1, 2):
         if g < 2:
             span = pl.ds(wide, narrow) if g == 0 else pl.ds(0, wide)
@@ -210,17 +235,11 @@
         if g == 0:
             rows[z, shared] = squeezed(wide)
         else:
-            for p in (2 * g - 2, 2 * g - 1):
-                rows[z, base + p] = squeezed(p * PW)
-        if g == 2:
-            for copy in ahead:
-                copy.wait_send()
+            rows[z, base + g - 1] = squeezed((g - 1) * PW)
         for way in (0, 1):
             z_send(z, way, 1, g)
-            ahead.append(sent.pop())
         share(z, 0, g)
 
-    sent.extend(ahead[4:])
     for copy in weights[:2]:
         copy.wait()
 
@@ -229,33 +248,42 @@
             return [0]
         return [2 * t - 1, 2 * t] if t < 4 else [7]
 
-    def work(i):
-        ready(blocks[i], i)
-        hidden(blocks[i])
-        core_push(blocks[i], i)
+    def work(group):
+        for i in group:
+            ready(blocks[i], i)
+        hidden(group)
+        for i in group:
+            core_push(blocks[i], i)
 
     for t in (1, 2, 3, 4):
-        for g in (0, 1, 2):
+        for g in (0, 1, 2) if t < 4 else (0, 2, 1):
             for way in (0, 1):
                 if not goes(way, t, g):
                     continue
                 i = group(t)[way] if t < 4 else 7
                 b = blocks[i]
-                arrive(parts_of(b, g), z_ss.at[way, t, g], z_rs.at[way, t, g])
+                arrive(z_part(b, way, t, g), z_ss.at[way, t, g], z_rs.at[way, t, g])
                 z_send(b, way, t + 1, g)
-                share(b, i, g)
-            if g == 0 and t >= 2:
-                for i in group(t - 2):
-                    spread(blocks[i], i)
-            if g == 1:
+                if t < 4 or g != 1 or way == 1:
+                    share(b, i, g)
+            if g == 0:
                 for i in group(t - 1):
-                    x_pass(blocks[i], i)
-            if 0 < g <= len(group(t - 1)):
-                work(group(t - 1)[g - 1])
-    x_pass(blocks[7], 7)
+                    x_near(blocks[i], i)
+                if t >= 3:
+                    for i in group(t - 3):
+                        spread(blocks[i], i)
+            if t >= 2 and g == 1:
+                work(group(t - 2))
+        for i in group(t - 1):
+            x_far(blocks[i], i)
+    for i in group(2):
+        spread(blocks[i], i)
+    x_near(blocks[7], 7)
+    x_far(blocks[7], 7)
+    work(group(3))
     for i in group(3):
         spread(blocks[i], i)
-    work(7)
+    work([7])
     spread(blocks[7], 7)
 
     remote(a2a_r.at[pl.ds(0, 31)], a2a_r.at[pl.ds(0, 31)], a_ss.at[0, 0], a_rs.at[0], sibling).wait_recv()
@@ -281,21 +309,20 @@
             for q in range(4):
                 back_s[n + 8 * q, r:r + 16, :] = (values[q] * FF ** -0.5).astype(BF16)
 
-    rot[z, x] = back_s[me32]
-    for dz in (4, 3, 5, 2, 6, 1, 7, 0):
+    opposite = mod(z + 4, NZ)
+    rot[opposite, x] = back_s[me32]
+    for dz in (0, 1, 7, 2, 6, 3, 5, 4):
         zz = mod(z + dz, NZ)
-        for j in range(NX):
+        for j in (2, 1, 3, 0):
             if dz + j:
                 s = zz * NX + x_peer[j]
-                push(back_s.at[s], rot.at[z, x], b_ss.at[dz, j], b_rs.at[z], at(x=x_peer[j], z=zz))
+                push(back_s.at[s], rot.at[opposite, x], b_ss.at[dz, j], b_rs.at[opposite], at(x=x_peer[j], z=zz))
 
     weights[2].wait()
     order = [4, 3, 5, 2, 6, 1, 7, 0]
-    x3_parts = [mod(x + i, NX) for i in range(NX)]
-
     def down_block(dz, turn):
         b = mod(z + dz, NZ)
-        if dz:
+        if dz != 4:
             arrive(rot.at[b], b_ss.at[0, 1], b_rs.at[b])
         else:
             arrive(rot.at[b, pl.ds(0, 3)], b_ss.at[0, 1], b_rs.at[b])
@@ -313,105 +340,142 @@
             columns = pl.ds(pl.multiple_of((2 * k + c) * SLICE, 128), SLICE)
             own[b, k] = jnp.dot(block, down[:, columns], preferred_element_type=F32)
 
+    def mine(b, k, h):
+        half = slice(HB * h, HB * h + HB)
+        return own[b, k, half, 0:PW] + sib_r[b, k, half, 0:PW]
+
+    def x_push(dz, n, value, j):
+        b = mod(z + dz, NZ)
+        xs[b, n] = value.astype(BF16)
+        push(xs.at[b, n], xr.at[b, n], x3_ss.at[dz, n], x3_rs.at[dz, n], at(x=x_peer[j]))
+
+    def x_arrive(dz, n):
+        arrive(xr.at[mod(z + dz, NZ), n], x3_ss.at[dz, n], x3_rs.at[dz, n])
+
     def x_scatter(dz):
         b = mod(z + dz, NZ)
         arrive(sib_r.at[b], sib_ss.at[0], sib_rs.at[dz])
-        for j in (2, 1, 3):
-            k = x3_parts[j]
-            xs[b, j] = (own[b, k, :, 0:PW] + sib_r[b, k, :, 0:PW]).astype(BF16)
-            push(xs.at[b, j], xr.at[b, j], x3_ss.at[dz, j], x3_rs.at[dz, j], at(x=k))
+        for h, j in ((0, 1), (1, 3)):
+            x_push(dz, h, mine(b, x_peer[2], h), j)
+        for h, j in ((0, 1), (1, 3)):
+            x_push(dz, 2 + h, mine(b, x_peer[j], 1 - h), j)
+
+    def x_relay(dz):
+        b = mod(z + dz, NZ)
+        for h, j in ((0, 1), (1, 3)):
+            x_arrive(dz, h)
+            x_push(dz, 4 + h, mine(b, x_peer[j], h) + xr[b, h].astype(F32), j)
+
+    def x_gathered(dz):
+        for n in (2, 3, 4, 5):
+            x_arrive(dz, n)
 
     def term(b, part):
         if part:
-            k = part - 1
-            return own[b, k, :, PW:] + sib_r[b, k, :, PW:]
-        total = own[b, x, :, 0:PW] + sib_r[b, x, :, 0:PW]
-        for j in range(1, NX):
-            total += xr[b, j].astype(F32)
-        return total
-
-    def x_gathered(dz):
-        b = mod(z + dz, NZ)
-        for j in range(1, NX):
-            arrive(xr.at[b, j], x3_ss.at[dz, j], x3_rs.at[dz, j])
-
-    def far(way, part):
-        return (part < 3) == (way == 0)
+            pair = (2 * part - 2, 2 * part - 1)
+            return jnp.concatenate([own[b, k, :, PW:] + sib_r[b, k, :, PW:] for k in pair], axis=1)
+        upper = mine(b, x, 0) + xr[b, 4].astype(F32) + xr[b, 3].astype(F32)
+        lower = mine(b, x, 1) + xr[b, 2].astype(F32) + xr[b, 5].astype(F32)
+        return jnp.concatenate([upper, lower], axis=0)
+
+    def span_of(way, step, part):
+        if step:
+            return slice(0, BLK)
+        if part:
+            return slice(0, BLK) if (part == 1) == (way == 0) else None
+        return slice(HB * way, HB * way + HB)
+
+    def z_ref(ref, way, step, part):
+        span = span_of(way, step, part)
+        return ref.at[way, step, part, pl.ds(span.start, span.stop - span.start)]
 
     def chain_in(way, step, part):
-        arrive(zr.at[way, step, part], z3_ss.at[way, step, part], z3_rs.at[way, step, part])
+        arrive(z_ref(zr, way, step, part), z3_ss.at[way, step, part], z3_rs.at[way, step, part])
 
     def chain(step, parts):
         for part in parts:
             for way in (0, 1):
-                if step == 0 and not far(way, part):
+                span = span_of(way, step, part)
+                if span is None:
                     continue
-                total = term(mod(z + (4 - step if way == 0 else 4 + step), NZ), part)
-                if step > 1 or (step == 1 and far(way, part)):
+                value = term(mod(z + (4 - step if way == 0 else 4 + step), NZ), part)
+                before = span_of(way, step - 1, part) if step else None
+                if before is not None:
                     chain_in(way, step - 1, part)
-                    total += zr[way, step - 1, part].astype(F32)
-                zs[way, step, part] = total.astype(BF16)
+                    came = zr[way, step - 1, part, before, :].astype(F32)
+                    pieces = [value[0:before.start], value[before] + came, value[before.stop:BLK]]
+                    value = jnp.concatenate([piece for piece in pieces if piece.shape[0]], axis=0)
+                zs[way, step, part, span, :] = value[span].astype(BF16)
                 push(
-                    zs.at[way, step, part], zr.at[way, step, part],
+                    z_ref(zs, way, step, part), z_ref(zr, way, step, part),
                     z3_ss.at[way, step, part], z3_rs.at[way, step, part], step_to[way],
                 )
 
     down_block(4, 0)
     down_block(3, 1)
     x_scatter(4)
-    chain(0, (1, 3, 2, 4))
+    chain(0, (1, 2))
     down_block(5, 2)
     x_scatter(3)
+    x_relay(4)
     down_block(2, 3)
     x_scatter(5)
+    x_relay(3)
     x_gathered(4)
     chain(0, (0,))
-    chain(1, (1, 2, 3, 4))
+    chain(1, (1, 2))
     down_block(6, 4)
     x_scatter(2)
+    x_relay(5)
     down_block(1, 5)
+    x_scatter(6)
+    x_relay(2)
     x_gathered(3)
     x_gathered(5)
     chain(1, (0,))
-    x_scatter(6)
-    chain(2, (1, 2, 3, 4))
+    chain(2, (1, 2))
     down_block(7, 6)
     x_scatter(1)
+    x_relay(6)
     down_block(0, 7)
+    x_scatter(7)
+    x_relay(1)
     x_gathered(2)
     x_gathered(6)
     chain(2, (0,))
-    x_scatter(7)
-    chain(3, (1, 2, 3, 4))
+    chain(3, (1, 2))
     x_scatter(0)
+    x_relay(7)
     x_gathered(1)
     x_gathered(7)
     chain(3, (0,))
+    x_relay(0)
     x_gathered(0)
 
     def final(part):
         return term(z, part) + (zr[0, 3, part].astype(F32) + zr[1, 3, part].astype(F32))
 
-    for k in range(NX):
+    for part in (1, 2):
         for way in (0, 1):
-            chain_in(way, 3, 1 + k)
-        fxs[k] = final(1 + k).astype(BF16)
+            chain_in(way, 3, part)
+        total = final(part)
+        for k in (2 * part - 2, 2 * part - 1):
+            columns = slice(ZW * (k % 2), ZW * (k % 2) + ZW)
+            fxf[k] = total[:, columns]
+            fxs[k] = total[:, columns].astype(BF16)
     for j in (2, 1, 3):
-        k = x_peer[j]
-        push(fxs.at[k], fxr.at[j], fx_ss.at[j], fx_rs.at[j], at(x=k))
-
-    def y_send(half):
+        push(fxs.at[x_peer[j]], fxr.at[j], fx_ss.at[j], fx_rs.at[j], at(x=x_peer[j]))
+
+    def y_send(half, src, dst):
         for i in (2, 1, 3):
             span = pl.ds(pl.multiple_of(y_peer[i] * CAP, 8), CAP)
-            push(ys.at[half, span], yr.at[half, y], y3_ss.at[half, i], y3_rs.at[half, i], at(y=y_peer[i]))
-        yr[half, y] = ys[half, pl.ds(pl.multiple_of(y * CAP, 8), CAP)]
+            push(src.at[span], dst.at[y], y3_ss.at[half, i], y3_rs.at[half, i], at(y=y_peer[i]))
+        dst[y] = src[pl.ds(pl.multiple_of(y * CAP, 8), CAP)]
 
     for way in (0, 1):
         chain_in(way, 3, 0)
-    ys[0] = final(0)
-    y_send(0)
-    total = own[z, x, :, PW:] + sib_r[z, x, :, PW:]
-    total += zr[0, 3, 1 + x].astype(F32) + zr[1, 3, 1 + x].astype(F32)
+    ysa[...] = final(0)
+    y_send(0, ysa, yra)
 
     logits = [column(router_logits[e:e + 1, :]) for e in range(EXPERTS)]
     picked = []
@@ -424,17 +488,18 @@
     expert, placed = place(CAP)
     combine = jnp.where(placed, jnp.where(first == expert, share0, 1.0 - share0), 0.0)
 
+    total = fxf[x]
     for j in range(1, NX):
         arrive(fxr.at[j], fx_ss.at[j], fx_rs.at[j])
         total += fxr[j].astype(F32)
-    ys[1] = total
-    y_send(1)
-    for half in (0, 1):
+    ysb[...] = total
+    y_send(1, ysb, yrb)
+    for half, dst, columns in ((0, yra, slice(0, PW)), (1, yrb, slice(PW, SLICE))):
         for i in range(1, NY):
-            source = y_peer[NY - i]
-            arrive(yr.at[half, source], y3_ss.at[half, i], y3_rs.at[half, i])
-        out[:, half * PW:(half + 1) * PW] = jnp.dot(
-            combine, yr[half].reshape(EXPERTS * CAP, PW), precision=lax.Precision.HIGHEST, preferred_element_type=F32
+            arrive(dst.at[y_peer[NY - i]], y3_ss.at[half, i], y3_rs.at[half, i])
+        returned = dst[...].reshape(EXPERTS * CAP, columns.stop - columns.start)
+        out[:, columns] = jnp.dot(
+            combine, returned, precision=lax.Precision.HIGHEST, preferred_element_type=F32
         ).astype(BF16)
     for copy in sent:
         copy.wait_send()
@@ -445,10 +510,10 @@
 def run(tokens, expert_ids, router_logits, gate_weight, up_weight, down_weight):
     vmem, dma = pltpu.VMEM, pltpu.SemaphoreType.DMA
     scratch = [
-        vmem((TOK, D), BF16), vmem((EXPERTS * TOK, 5 * PW), BF16),
+        vmem((TOK, D), BF16), vmem((EXPERTS * TOK, 3 * PW), BF16),
         vmem((D, UNITS), BF16), vmem((D, UNITS), BF16), vmem((UNITS, D), BF16),
         vmem((UNITS, UNITS), BF16),
-        vmem((NY, TOK, 5 * PW), BF16),
+        vmem((NY, TOK, 3 * PW), BF16),
         vmem((NZ, PARTS, BLK, PW), BF16),
         vmem((NZ, BLK, UNITS), F32), vmem((NZ, BLK, UNITS), F32),
         vmem((NZ, NX, 48, 128), BF16),
@@ -458,10 +523,11 @@
         vmem((NZ, NX, BLK, SLICE), F32),
         vmem((2, NX, BLK, SLICE), F32),
         vmem((NZ, NX, BLK, SLICE), F32),
-        vmem((NZ, NX, BLK, PW), BF16), vmem((NZ, NX, BLK, PW), BF16),
-        vmem((2, 4, 5, BLK, PW), BF16), vmem((2, 4, 5, BLK, PW), BF16),
-        vmem((NX, BLK, PW), BF16), vmem((NX, BLK, PW), BF16),
-        vmem((2, BLK, PW), F32), vmem((2, NY, CAP, PW), F32),
+        vmem((NZ, 6, HB, PW), BF16), vmem((NZ, 6, HB, PW), BF16),
+        vmem((2, 4, 3, BLK, PW), BF16), vmem((2, 4, 3, BLK, PW), BF16),
+        vmem((NX, BLK, ZW), F32), vmem((NX, BLK, ZW), BF16), vmem((NX, BLK, ZW), BF16),
+        vmem((BLK, PW), F32), vmem((BLK, ZW), F32),
+        vmem((NY, CAP, PW), F32), vmem((NY, CAP, ZW), F32),
         dma, dma((3,)),
         dma((NY, 2)), dma((NY, 2)),
         dma((2, 5, 3)), dma((2, 5, 3)),
@@ -471,8 +537,8 @@
         dma((NZ, NX)), dma((1,)),
         dma((NZ, NX)), dma((NZ,)),
         dma((2,)), dma((NZ,)),
-        dma((NZ, NX)), dma((NZ, NX)),
-        dma((2, 4, 5)), dma((2, 4, 5)),
+        dma((NZ, 6)), dma((NZ, 6)),
+        dma((2, 4, 3)), dma((2, 4, 3)),
         dma((NX,)), dma((NX,)),
         dma((2, NY)), dma((2, NY)),
     ]

time: 122 us -> 113 us (0.926); the launches traced: 120 us -> 112 us
  Pallas kernels: 119 us -> 111 us
    pallas_call x1, Pallas kernels: 119 us -> 111 us  [run(): pl.pallas_call(kernel, out_shape=jax.ShapeDtypeStruct((TOK, SLICE), BF16)...]
where the time goes in v3:
time: 113 us; the launch traced here: 112 us
  Pallas kernels  111 us (98%)
  local copies, waits for them, and re-layouts  1.42 us (1%)
    pallas_call x1, Pallas kernels, run(): pl.pallas_call(kernel, out_shape=jax.ShapeDtypeStruct((TOK, SLICE), BF16)...  111 us

profile of v3, /device:TPU:8, one launch (start us, length us, event | category | flops | bytes accessed | tf_op | source)
XLA Modules:
  0.0 112.5 jit_solution(10791986813366298142)
XLA Ops:
  0.0 111.0 %experts.1 = bf16[32,768]{1,0:T(8,128)(2,1)} custom-call(bf16[32,6144]{1,0:T(8,128)(2,1)} %tokens_hbm.1, s32[2,32]{1,0:T(2,128)} %bitcast.3, f32[4,32]{1,0:T(4,128)} %bitcast.2, bf16[1,6144,256]{2,1,0:T(8,128)(2,1)} %gate_hbm.1, bf16[1,6144,256]{2,1,0:T(8,128)(2,1)} %up_hbm.1, bf16[1,256,6144]{2,1,0:T(8,128)(2,1)} %down_hbm.1), custom_call_target="tpu_custom_call" | custom-call | tf_op jit(solution)/shard_map/experts/pallas_call | solution.py:545
  111.1 1.4 %copy.8 = bf16[32,768]{1,0:T(8,128)(2,1)} copy(bf16[32,768]{1,0:T(8,128)(2,1)} %experts.1) | data formatting | bytes 98304

commit v4 on v3

--- a/solution.py
+++ b/solution.py
@@ -267,15 +267,18 @@
                 if t < 4 or g != 1 or way == 1:
                     share(b, i, g)
             if g == 0:
+                if t >= 2:
+                    for i in group(t - 2):
+                        x_far(blocks[i], i)
                 for i in group(t - 1):
                     x_near(blocks[i], i)
                 if t >= 3:
                     for i in group(t - 3):
                         spread(blocks[i], i)
-            if t >= 2 and g == 1:
+            if t >= 2 and g == 2:
                 work(group(t - 2))
-        for i in group(t - 1):
-            x_far(blocks[i], i)
+    for i in group(3):
+        x_far(blocks[i], i)
     for i in group(2):
         spread(blocks[i], i)
     x_near(blocks[7], 7)

time: 113 us -> 111 us (0.982)
    pallas_call x1, Pallas kernels: 111 us -> 110 us  [run(): pl.pallas_call(kernel, out_shape=jax.ShapeDtypeStruct((TOK, SLICE), BF16)...]
where the time goes in v4:
time: 111 us
  Pallas kernels  110 us (99%)
  local copies, waits for them, and re-layouts  1.42 us (1%)
    pallas_call x1, Pallas kernels, run(): pl.pallas_call(kernel, out_shape=jax.ShapeDtypeStruct((TOK, SLICE), BF16)...  110 us

profile of v4, /device:TPU:8, one launch (start us, length us, event | category | flops | bytes accessed | tf_op | source)
XLA Modules:
  0.0 111.3 jit_solution(15202424364519404335)
XLA Ops:
  0.0 109.9 %experts.1 = bf16[32,768]{1,0:T(8,128)(2,1)} custom-call(bf16[32,6144]{1,0:T(8,128)(2,1)} %tokens_hbm.1, s32[2,32]{1,0:T(2,128)} %bitcast.3, f32[4,32]{1,0:T(4,128)} %bitcast.2, bf16[1,6144,256]{2,1,0:T(8,128)(2,1)} %gate_hbm.1, bf16[1,6144,256]{2,1,0:T(8,128)(2,1)} %up_hbm.1, bf16[1,256,6144]{2,1,0:T(8,128)(2,1)} %down_hbm.1), custom_call_target="tpu_custom_call" | custom-call | tf_op jit(solution)/shard_map/experts/pallas_call | solution.py:548
  109.9 1.4 %copy.8 = bf16[32,768]{1,0:T(8,128)(2,1)} copy(bf16[32,768]{1,0:T(8,128)(2,1)} %experts.1) | data formatting | bytes 98304

commit v5 on v4

--- a/solution.py
+++ b/solution.py
@@ -424,19 +424,19 @@
     down_block(2, 3)
     x_scatter(5)
     x_relay(3)
+    chain(1, (1, 2))
     x_gathered(4)
     chain(0, (0,))
-    chain(1, (1, 2))
     down_block(6, 4)
     x_scatter(2)
     x_relay(5)
     down_block(1, 5)
     x_scatter(6)
     x_relay(2)
+    chain(2, (1, 2))
     x_gathered(3)
     x_gathered(5)
     chain(1, (0,))
-    chain(2, (1, 2))
     down_block(7, 6)
     x_scatter(1)
     x_relay(6)

time: 111 us -> 111 us (level)
  no operation moved by 1% of the time
where the time goes in v5:
time: 111 us
  Pallas kernels  109 us (98%)
  local copies, waits for them, and re-layouts  1.42 us (1%)
    pallas_call x1, Pallas kernels, run(): pl.pallas_call(kernel, out_shape=jax.ShapeDtypeStruct((TOK, SLICE), BF16)...  109 us

profile of v5, /device:TPU:8, one launch (start us, length us, event | category | flops | bytes accessed | tf_op | source)
XLA Modules:
  0.0 110.6 jit_solution(10099993861559068251)
XLA Ops:
  0.0 109.1 %experts.1 = bf16[32,768]{1,0:T(8,128)(2,1)} custom-call(bf16[32,6144]{1,0:T(8,128)(2,1)} %tokens_hbm.1, s32[2,32]{1,0:T(2,128)} %bitcast.3, f32[4,32]{1,0:T(4,128)} %bitcast.2, bf16[1,6144,256]{2,1,0:T(8,128)(2,1)} %gate_hbm.1, bf16[1,6144,256]{2,1,0:T(8,128)(2,1)} %up_hbm.1, bf16[1,256,6144]{2,1,0:T(8,128)(2,1)} %down_hbm.1), custom_call_target="tpu_custom_call" | custom-call | tf_op jit(solution)/shard_map/experts/pallas_call | solution.py:548
  109.2 1.4 %copy.8 = bf16[32,768]{1,0:T(8,128)(2,1)} copy(bf16[32,768]{1,0:T(8,128)(2,1)} %experts.1) | data formatting | bytes 98304
